TPU v7x, 1024 devices: a whole 4x4x32 slice. The times are simulated.
1024 devices in a mesh: horiz: 128 (over y, z), lev: 8 (over x, core).
Axes of the slice: x: 4, y: 4, z: 32, core: 2. Of those that a mesh axis runs over, the one named last changes fastest.
Arguments:
- atm_state: float32 [4, 16, 16, 32768], P(None, 'lev', None, 'horiz'), may hold values from -6 to 6
- atm_mixing: float32 [4, 16], P(None, 'lev'), may hold values from 0.05 to 0.45
- element_operator: float32 [16, 16], replicated, may hold values from -1.5 to 1.5
- ocean_state: float32 [2, 16, 524288], P(None, 'lev', 'horiz'), may hold values from -6 to 6
- ocean_mixing: float32 [2, 16], P(None, 'lev'), may hold values from 0.05 to 0.45
- atm_flux: bfloat16 [16, 32768], P(None, 'horiz'), may hold values from -6 to 6
- sea_temp: bfloat16 [524288], P('horiz'), may hold values from -6 to 6
- ocean_tiles: bfloat16 [10240, 128, 128], P(('horiz', 'lev')), may hold values from -0.5 to 0.5
- ocean_tile_src: int32 [10240], P(('horiz', 'lev')), may hold values from 0 to 31
- ocean_tile_dst: int32 [10240], P(('horiz', 'lev')), may hold values from 0 to 32, as said below
- atmos_tiles: bfloat16 [10240, 128, 128], P(('horiz', 'lev')), may hold values from -0.5 to 0.5
- atmos_tile_src: int32 [10240], P(('horiz', 'lev')), may hold values from 0 to 31
- atmos_tile_dst: int32 [10240], P(('horiz', 'lev')), may hold values from 0 to 32, as said below
Outputs:
- atm_next: float32 [4, 16, 16, 32768], P(None, 'lev', None, 'horiz')
- ocean_next: float32 [2, 16, 524288], P(None, 'lev', 'horiz')
Inputs may be any that keep to these rules, and one draw needn't show every extreme that they name: `ocean_tile_dst`: entry i of a receiver h, l describes the inbound slot from sender (h - (o - 2)) mod 128, l, reach o, place c; it names a local ocean block, or 32 for an empty slot; every local ocean block is named by at least one entry of each receiver h. `atmos_tile_dst`: entry i of a receiver h, l describes the inbound slot from sender (h - (o - 2)) mod 128, l, reach o, place c; it names a local atmosphere block, or 32 for an empty slot; every local atmosphere block is named by at least one entry of each receiver h.
All inputs are finite; a program needn't handle non-finite values.
Results may differ from a plain program's by a relative error of at most 0.00045.
Values may be sent and summed in bfloat16 or wider, within the bound.
No kernel may reach another device: no remote copies, remote signals or barrier semaphores. Data moves between devices by JAX's collectives and lax.ppermute only.
A program may use at most 32 MiB of HBM per device.

v0:
```python
import jax
import jax.numpy as jnp
from jax import lax
from jax.sharding import PartitionSpec as P

BLOCK = 128
NEAR = 2
CAP = 2


def padded_2(cells, sides, width):
    for axis, dim in sides:
        count = lax.axis_size(axis)
        ends = count - 1
        head = lax.slice_in_dim(cells, 0, width, axis=dim)
        tail = lax.slice_in_dim(cells, cells.shape[dim] - width, cells.shape[dim], axis=dim)
        cells = jnp.concatenate(
            [
                lax.ppermute(tail, axis, [(i, (i + 1) % count) for i in range(ends)]),
                cells,
                lax.ppermute(head, axis, [((i + 1) % count, i) for i in range(ends)]),
            ],
            axis=dim,
        )
    return cells


def shifted(value, axis, steps):
    count = lax.axis_size(axis)
    pairs = [(source, (source + steps) % count) for source in range(count)]
    return lax.ppermute(value, axis, pairs)


def vertical(fields, mixing):
    padded = padded_2(fields, (("lev", 1),), 1)
    beneath = padded[:, :-2]
    overhead = padded[:, 2:]
    at_bottom = lax.axis_index("lev") == 0
    at_top = lax.axis_index("lev") == lax.axis_size("lev") - 1
    beneath = beneath.at[:, 0].set(jnp.where(at_bottom, fields[:, 0], beneath[:, 0]))
    overhead = overhead.at[:, -1].set(jnp.where(at_top, fields[:, -1], overhead[:, -1]))
    mix_rate = mixing.reshape(mixing.shape + (1,) * (fields.ndim - 2))
    return fields + mix_rate * (overhead - 2.0 * fields + beneath)


def tile_products(tile_mats, sources, blocks):
    picked = blocks[sources]
    result = jnp.einsum("tij,tj->ti", tile_mats, picked, preferred_element_type=jnp.float32)
    return result.astype(jnp.bfloat16).reshape(2 * NEAR + 1, CAP, BLOCK)


def gather_blocks(inbound, dest_ids, out_blocks):
    labels = jnp.arange(out_blocks, dtype=jnp.int32)
    onehot = (dest_ids[None, :] == labels[:, None]).astype(jnp.bfloat16)
    return jnp.dot(onehot, inbound.reshape(-1, BLOCK), preferred_element_type=jnp.float32)


def shards(
    atm_state,
    atm_mixing,
    element_operator,
    ocean_state,
    ocean_mixing,
    atm_flux,
    sea_temp,
    ocean_tiles,
    ocean_tile_src,
    ocean_tile_dst,
    atmos_tiles,
    atmos_tile_src,
    atmos_tile_dst,
):
    reach = 2 * NEAR + 1
    at_bottom = lax.axis_index("lev") == 0
    ocean_blocks = ocean_state.shape[2] // BLOCK
    atmos_blocks = atm_flux.shape[0] * atm_flux.shape[1] // BLOCK
    atm_blocks = atm_flux.reshape(-1, BLOCK)
    sea_blocks = sea_temp.reshape(-1, BLOCK)
    to_ocean = tile_products(ocean_tiles, ocean_tile_src, atm_blocks)
    to_atmos = tile_products(atmos_tiles, atmos_tile_src, sea_blocks)
    payload = jnp.stack([to_ocean, to_atmos], axis=1)
    inbound = jnp.stack(
        [
            (
                payload[offset_idx]
                if offset_idx == NEAR
                else shifted(payload[offset_idx], "horiz", offset_idx - NEAR)
            )
            for offset_idx in range(reach)
        ],
        axis=0,
    )
    heat_part = gather_blocks(inbound[:, 0], ocean_tile_dst, ocean_blocks).reshape(-1)
    temp_part = gather_blocks(inbound[:, 1], atmos_tile_dst, atmos_blocks).reshape(atm_flux.shape)
    heat_in, temp_in = lax.psum((heat_part, temp_part), "lev")
    mixed = vertical(atm_state, atm_mixing)
    lateral = jnp.einsum("ij,fkje->fkie", element_operator, mixed, precision=lax.Precision.HIGHEST)
    atm_next = mixed + 0.25 * lateral
    atm_next = atm_next.at[2, 0].add(jnp.where(at_bottom, 0.5 * temp_in, 0.0))
    ocean_next = vertical(ocean_state, ocean_mixing)
    ocean_next = ocean_next.at[0, 0].add(jnp.where(at_bottom, 0.5 * heat_in, 0.0))
    return (atm_next, ocean_next)


def solution(mesh):
    placed = (
        P(None, "lev", None, "horiz"),
        P(None, "lev"),
        P(),
        P(None, "lev", "horiz"),
        P(None, "lev"),
        P(None, "horiz"),
        P("horiz"),
        P(("horiz", "lev"), None, None),
        P(("horiz", "lev")),
        P(("horiz", "lev")),
        P(("horiz", "lev"), None, None),
        P(("horiz", "lev")),
        P(("horiz", "lev")),
    )
    return jax.shard_map(
        shards,
        mesh=mesh,
        in_specs=placed,
        out_specs=(P(None, "lev", None, "horiz"), P(None, "lev", "horiz")),
        check_vma=False,
    )
```

profile of v0, /device:TPU:32, one launch (start us, length us, event | category | flops | bytes accessed | tf_op | source)
XLA Modules:
  0.0 75.9 jit_solution(12132874205433619538)
XLA Ops:
  0.7 0.9 %fusion.19 = (f32[4,1,16,256]{3,2,1,0:T(8,128)S(1)}, f32[4,1,16,256]{3,2,1,0:T(8,128)S(1)}) fusion(f32[4,2,16,256]{3,2,1,0:T(8,128)} %param.25), kind=kLoop, calls=%fused_computation.55 | loop fusion | bytes 262144 | tf_op jit(solution)/shard_map/slice | solution.py:15
  1.6 1.3 %collective-permute-start = (f32[4,1,16,256]{3,2,1,0:T(8,128)S(1)}, f32[4,1,16,256]{3,2,1,0:T(8,128)S(1)}, u32[]{:S(2)}, u32[]{:S(2)}) collective-permute-start(f32[4,1,16,256]{3,2,1,0:T(8,128)S(1)} %get-tuple-element.80), channel_id=1, source_target_pairs={{1,0},{2,1},{3,2},{4,3},{5,4},{6,5},{7,6},{9,8},{10,9},{11,10},{12... | collective-permute-start | bytes 196616 | tf_op jit(solution)/shard_map/ppermute | solution.py:21
  2.9 3.0 %collective-permute-start.1 = (f32[4,1,16,256]{3,2,1,0:T(8,128)S(1)}, f32[4,1,16,256]{3,2,1,0:T(8,128)S(1)}, u32[]{:S(2)}, u32[]{:S(2)}) collective-permute-start(f32[4,1,16,256]{3,2,1,0:T(8,128)S(1)} %get-tuple-element.81), channel_id=1, source_target_pairs={{0,1},{1,2},{2,3},{3,4},{4,5},{5,6},{6,7},{8,9},{9,10},{10,11},{11... | collective-permute-start | bytes 196616 | tf_op jit(solution)/shard_map/ppermute | solution.py:19
  5.9 0.7 reshape.216
  6.7 0.7 compare_select_fusion
  7.3 0.6 gather_fusion
  7.9 0.3 fusion.16
  8.3 0.7 copy-done.5
  8.9 0.6 gather_fusion.1
  9.5 0.3 fusion.14
  9.8 20.7 %collective-permute-start.2 = (bf16[2,2,128]{2,1,0:T(2,128)(2,1)S(1)}, bf16[2,2,128]{2,1,0:T(2,128)(2,1)S(1)}, u32[]{:S(2)}, u32[]{:S(2)}) collective-permute-start(bf16[2,2,128]{2,1,0:T(2,128)(2,1)S(1)} %get-tuple-element.92), channel_id=1, source_target_pairs={{0,1008},{8,1016},{16,0},{24,8},{32,16},{40,24},{48,32},{56,40},{6... | collective-permute-start | bytes 3080 | tf_op jit(solution)/shard_map/ppermute | solution.py:31
  30.5 2.9 %collective-permute-start.3 = (bf16[2,2,128]{2,1,0:T(2,128)(2,1)S(1)}, bf16[2,2,128]{2,1,0:T(2,128)(2,1)S(1)}, u32[]{:S(2)}, u32[]{:S(2)}) collective-permute-start(bf16[2,2,128]{2,1,0:T(2,128)(2,1)S(1)} %get-tuple-element.91), channel_id=1, source_target_pairs={{0,1016},{8,0},{16,8},{24,16},{32,24},{40,32},{48,40},{56,48},{64,... | collective-permute-start | bytes 3080 | tf_op jit(solution)/shard_map/ppermute | solution.py:31
  33.5 2.9 %collective-permute-start.4 = (bf16[2,2,128]{2,1,0:T(2,128)(2,1)S(1)}, bf16[2,2,128]{2,1,0:T(2,128)(2,1)S(1)}, u32[]{:S(2)}, u32[]{:S(2)}) collective-permute-start(bf16[2,2,128]{2,1,0:T(2,128)(2,1)S(1)} %get-tuple-element.93), channel_id=1, source_target_pairs={{0,8},{8,16},{16,24},{24,32},{32,40},{40,48},{48,56},{56,64},{64,7... | collective-permute-start | bytes 3080 | tf_op jit(solution)/shard_map/ppermute | solution.py:31
  36.5 0.7 copy-done.9
  37.2 1.9 %collective-permute-start.5 = (bf16[2,2,128]{2,1,0:T(2,128)(2,1)S(1)}, bf16[2,2,128]{2,1,0:T(2,128)(2,1)S(1)}, u32[]{:S(2)}, u32[]{:S(2)}) collective-permute-start(bf16[2,2,128]{2,1,0:T(2,128)(2,1)S(1)} %get-tuple-element.90), channel_id=1, source_target_pairs={{0,16},{8,24},{16,32},{24,40},{32,48},{40,56},{48,64},{56,72},{64,... | collective-permute-start | bytes 3080 | tf_op jit(solution)/shard_map/ppermute | solution.py:31
  39.2 1.3 %collective-permute-start.6 = (f32[2,1,4096]{2,1,0:T(1,128)S(1)}, f32[2,1,4096]{2,1,0:T(1,128)S(1)}, u32[]{:S(2)}, u32[]{:S(2)}) collective-permute-start(f32[2,1,4096]{2,1,0:T(1,128)S(1)} %get-tuple-element.86), channel_id=1, source_target_pairs={{1,0},{2,1},{3,2},{4,3},{5,4},{6,5},{7,6},{9,8},{10,9},{11,10},{12... | collective-permute-start | bytes 98312 | tf_op jit(solution)/shard_map/ppermute | solution.py:21
  40.5 3.0 %collective-permute-start.7 = (f32[2,1,4096]{2,1,0:T(1,128)S(1)}, f32[2,1,4096]{2,1,0:T(1,128)S(1)}, u32[]{:S(2)}, u32[]{:S(2)}) collective-permute-start(f32[2,1,4096]{2,1,0:T(1,128)S(1)} %get-tuple-element.87), channel_id=1, source_target_pairs={{0,1},{1,2},{2,3},{3,4},{4,5},{5,6},{6,7},{8,9},{9,10},{10,11},{11... | collective-permute-start | bytes 98312 | tf_op jit(solution)/shard_map/ppermute | solution.py:19
  43.6 3.3 %collective-permute-done.5 = bf16[2,2,128]{2,1,0:T(2,128)(2,1)S(1)} collective-permute-done((bf16[2,2,128]{2,1,0:T(2,128)(2,1)S(1)}, bf16[2,2,128]{2,1,0:T(2,128)(2,1)S(1)}, u32[]{:S(2)}, u32[]{:S(2)}) %collective-permute-start.5) | collective-permute-done | bytes 1056 | tf_op jit(solution)/shard_map/ppermute | solution.py:31
  47.0 0.6 copy-done.10
  47.6 0.1 fusion.10
  47.7 0.6 copy-done.11
  48.4 0.1 convolution_bitcast_fusion
  48.5 23.6 %all-reduce = (f32[16,256]{1,0:T(8,128)S(1)}, f32[4096]{0:T(1024)S(1)}) all-reduce(f32[16,256]{1,0:T(8,128)S(1)} %reshape.218, f32[4096]{0:T(1024)S(1)} %convolution_bitcast_fusion), channel_id=1, replica_groups=mesh['horiz'=128,'lev'=8] {'lev'}, use_global_device_ids=true, to_apply=%region_0.0 | all-reduce | flops 8192 | bytes 65536 | tf_op jit(solution)/shard_map/psum | solution.py:95
  72.1 0.1 pad_maximum_fusion.3
  72.4 0.2 scatter.19
  72.6 0.2 scatter.16
  72.9 0.4 copy-done.8
  73.4 0.2 scatter-add.9
  73.6 0.6 copy-done.1
  74.3 0.7 copy-done.7
  74.9 0.3 fusion.1
  75.3 0.6 copy-done.4
  (50 shorter events, 0.7 us)
Async XLA Ops:
  0.6 7.3 %copy-start = (bf16[10,128,128]{2,1,0:T(8,128)(2,1)S(1)}, bf16[10,128,128]{2,1,0:T(8,128)(2,1)}, u32[]{:S(2)}) copy-start(bf16[10,128,128]{2,1,0:T(8,128)(2,1)} %param.32) | copy-start | bytes 983044
  0.6 8.8 %copy-start.3 = (bf16[10,128,128]{2,1,0:T(8,128)(2,1)S(1)}, bf16[10,128,128]{2,1,0:T(8,128)(2,1)}, u32[]{:S(2)}) copy-start(bf16[10,128,128]{2,1,0:T(8,128)(2,1)} %param.35) | copy-start | bytes 983044
  1.6 72.0 %collective-permute-start = (f32[4,1,16,256]{3,2,1,0:T(8,128)S(1)}, f32[4,1,16,256]{3,2,1,0:T(8,128)S(1)}, u32[]{:S(2)}, u32[]{:S(2)}) collective-permute-start(f32[4,1,16,256]{3,2,1,0:T(8,128)S(1)} %get-tuple-element.80), channel_id=1, source_target_pairs={{1,0},{2,1},{3,2},{4,3},{5,4},{6,5},{7,6},{9,8},{10,9},{11,10},{12... | collective-permute-start | bytes 196616 | tf_op jit(solution)/shard_map/ppermute | solution.py:21
  2.9 70.7 %collective-permute-start.1 = (f32[4,1,16,256]{3,2,1,0:T(8,128)S(1)}, f32[4,1,16,256]{3,2,1,0:T(8,128)S(1)}, u32[]{:S(2)}, u32[]{:S(2)}) collective-permute-start(f32[4,1,16,256]{3,2,1,0:T(8,128)S(1)} %get-tuple-element.81), channel_id=1, source_target_pairs={{0,1},{1,2},{2,3},{3,4},{4,5},{5,6},{6,7},{8,9},{9,10},{10,11},{11... | collective-permute-start | bytes 196616 | tf_op jit(solution)/shard_map/ppermute | solution.py:19
  8.2 0.7 copy-start.5
  9.5 26.9 %copy-start.2 = (f32[2,2,4096]{2,1,0:T(2,128)S(1)}, f32[2,2,4096]{2,1,0:T(2,128)}, u32[]{:S(2)}) copy-start(f32[2,2,4096]{2,1,0:T(2,128)} %param.28) | copy-start | bytes 196612
  9.8 27.4 %collective-permute-start.2 = (bf16[2,2,128]{2,1,0:T(2,128)(2,1)S(1)}, bf16[2,2,128]{2,1,0:T(2,128)(2,1)S(1)}, u32[]{:S(2)}, u32[]{:S(2)}) collective-permute-start(bf16[2,2,128]{2,1,0:T(2,128)(2,1)S(1)} %get-tuple-element.92), channel_id=1, source_target_pairs={{0,1008},{8,1016},{16,0},{24,8},{32,16},{40,24},{48,32},{56,40},{6... | collective-permute-start | bytes 3080 | tf_op jit(solution)/shard_map/ppermute | solution.py:31
  30.5 8.6 %collective-permute-start.3 = (bf16[2,2,128]{2,1,0:T(2,128)(2,1)S(1)}, bf16[2,2,128]{2,1,0:T(2,128)(2,1)S(1)}, u32[]{:S(2)}, u32[]{:S(2)}) collective-permute-start(bf16[2,2,128]{2,1,0:T(2,128)(2,1)S(1)} %get-tuple-element.91), channel_id=1, source_target_pairs={{0,1016},{8,0},{16,8},{24,16},{32,24},{40,32},{48,40},{56,48},{64,... | collective-permute-start | bytes 3080 | tf_op jit(solution)/shard_map/ppermute | solution.py:31
  33.5 7.1 %collective-permute-start.4 = (bf16[2,2,128]{2,1,0:T(2,128)(2,1)S(1)}, bf16[2,2,128]{2,1,0:T(2,128)(2,1)S(1)}, u32[]{:S(2)}, u32[]{:S(2)}) collective-permute-start(bf16[2,2,128]{2,1,0:T(2,128)(2,1)S(1)} %get-tuple-element.93), channel_id=1, source_target_pairs={{0,8},{8,16},{16,24},{24,32},{32,40},{40,48},{48,56},{56,64},{64,7... | collective-permute-start | bytes 3080 | tf_op jit(solution)/shard_map/ppermute | solution.py:31
  36.5 0.7 copy-start.9
  37.2 9.7 %collective-permute-start.5 = (bf16[2,2,128]{2,1,0:T(2,128)(2,1)S(1)}, bf16[2,2,128]{2,1,0:T(2,128)(2,1)S(1)}, u32[]{:S(2)}, u32[]{:S(2)}) collective-permute-start(bf16[2,2,128]{2,1,0:T(2,128)(2,1)S(1)} %get-tuple-element.90), channel_id=1, source_target_pairs={{0,16},{8,24},{16,32},{24,40},{32,48},{40,56},{48,64},{56,72},{64,... | collective-permute-start | bytes 3080 | tf_op jit(solution)/shard_map/ppermute | solution.py:31
  39.2 32.9 %collective-permute-start.6 = (f32[2,1,4096]{2,1,0:T(1,128)S(1)}, f32[2,1,4096]{2,1,0:T(1,128)S(1)}, u32[]{:S(2)}, u32[]{:S(2)}) collective-permute-start(f32[2,1,4096]{2,1,0:T(1,128)S(1)} %get-tuple-element.86), channel_id=1, source_target_pairs={{1,0},{2,1},{3,2},{4,3},{5,4},{6,5},{7,6},{9,8},{10,9},{11,10},{12... | collective-permute-start | bytes 98312 | tf_op jit(solution)/shard_map/ppermute | solution.py:21
  40.5 31.6 %collective-permute-start.7 = (f32[2,1,4096]{2,1,0:T(1,128)S(1)}, f32[2,1,4096]{2,1,0:T(1,128)S(1)}, u32[]{:S(2)}, u32[]{:S(2)}) collective-permute-start(f32[2,1,4096]{2,1,0:T(1,128)S(1)} %get-tuple-element.87), channel_id=1, source_target_pairs={{0,1},{1,2},{2,3},{3,4},{4,5},{5,6},{6,7},{8,9},{9,10},{10,11},{11... | collective-permute-start | bytes 98312 | tf_op jit(solution)/shard_map/ppermute | solution.py:19
  46.9 0.7 copy-start.10
  47.7 0.7 copy-start.11
  72.6 0.7 copy-start.8
  73.3 0.9 %copy-start.1 = (f32[4,2,16,256]{3,2,1,0:T(8,128)S(1)}, f32[4,2,16,256]{3,2,1,0:T(8,128)}, u32[]{:S(2)}) copy-start(f32[4,2,16,256]{3,2,1,0:T(8,128)} %param.25) | copy-start | bytes 393220
  73.6 0.6 copy-start.6
  74.2 0.7 copy-start.7
  75.3 0.7 copy-start.4
where the time goes:
time: 76.5 us; the launch traced here: 75.9 us
  starting transfers between devices  37.1 us (48%)
  blocking collectives  23.6 us (31%)
  local copies, waits for them, and re-layouts  8.71 us (11%)
  waiting for transfers between devices  3.36 us (4%)
  matrix products  1.12 us (1%)
  other arithmetic  1.05 us (1%)
  between operations  1.01 us (1%)
    ppermute x4, starting transfers between devices, shifted(): return lax.ppermute(value, axis, pairs)  28.4 us
    psum x1, blocking collectives, shards(): heat_in, temp_in = lax.psum((heat_part, temp_part), 'lev')  23.6 us
    ppermute x2, starting transfers between devices, padded_2(): lax.ppermute(tail, axis, [(i, (i + 1) % count) for i in range(ends)])  6.07 us
    unnamed x30, local copies, waits for them, and re-layouts  5.1 us
    ppermute x4, waiting for transfers between devices, shifted(): return lax.ppermute(value, axis, pairs)  3.35 us
    ppermute x2, starting transfers between devices, padded_2(): lax.ppermute(head, axis, [((i + 1) % count, i) for i in range(ends)])  2.58 us
  transfers between devices with their start and end apart: 8, of which 1 were waited for; matrix products, arithmetic and copies ran while one was open for 6% of the time, Pallas kernels for 0%

commit v1 on v0

v1 whole, which is shorter than its diff:
```python
import jax
import jax.numpy as jnp
from jax import lax
from jax.experimental import pallas as pl
from jax.experimental.pallas import tpu as pltpu
from jax.sharding import PartitionSpec as P

BLOCK = 128
NEAR = 2
CAP = 2
REACH = 2 * NEAR + 1
LANE = {0: 1, 1: 2, 2: 0, 3: 3, 4: 4}
EMPTY = 64


def prep_kernel(
    ocean_src, ocean_dst, atmos_src, atmos_dst,
    atm, ocean, flux, sea, ocean_tiles, atmos_tiles,
    send, up, down, picks,
):
    level = lax.axis_index("lev")
    picks[0:16] = flux[:, 0:128].astype(jnp.float32)
    picks[16:32] = flux[:, 128:256].astype(jnp.float32)
    picks[32:64] = sea[...].astype(jnp.float32)
    send[...] = jnp.zeros_like(send)
    for slot in range(REACH * CAP):
        reach, place = slot // CAP, slot % CAP
        base = 8 * LANE[reach]
        source = ocean_src[slot]
        row = picks[pl.ds((source % 2) * 16 + source // 2, 1), :].astype(jnp.bfloat16)
        product = lax.dot_general(
            row, ocean_tiles[slot], (((1,), (1,)), ((), ())), preferred_element_type=jnp.float32
        )
        send[base + place : base + place + 1] = product.astype(jnp.bfloat16).astype(jnp.float32)
        source = atmos_src[slot]
        row = picks[pl.ds(32 + source, 1), :].astype(jnp.bfloat16)
        product = lax.dot_general(
            row, atmos_tiles[slot], (((1,), (1,)), ((), ())), preferred_element_type=jnp.float32
        )
        send[base + 2 + place : base + 3 + place] = product.astype(jnp.bfloat16).astype(jnp.float32)
    lane = lax.broadcasted_iota(jnp.int32, (4, 128), 1)
    line = lax.broadcasted_iota(jnp.int32, (4, 128), 0)
    inside = lane % 64 - 8 * level
    codes = jnp.where((inside >= 4) & (inside < 8), EMPTY, 0)
    for slot in range(REACH * CAP):
        reach, place = slot // CAP, slot % CAP
        here = (line == reach // 2) & (lane // 64 == reach % 2)
        to = ocean_dst[slot]
        codes = jnp.where(here & (inside == place), jnp.where(to < 32, to, EMPTY), codes)
        to = atmos_dst[slot]
        code = jnp.where(to < 32, 32 + (to % 2) * 16 + to // 2, EMPTY)
        codes = jnp.where(here & (inside == 2 + place), code, codes)
    send[4:8] = codes.astype(jnp.float32)
    for field in range(4):
        rows = slice(16 * field, 16 * field + 16)
        more = slice(64 + 16 * field, 80 + 16 * field)
        up[rows] = atm[field, 1, :, 0:128]
        up[more] = atm[field, 1, :, 128:256]
        down[rows] = atm[field, 0, :, 0:128]
        down[more] = atm[field, 0, :, 128:256]
    down[128:192] = ocean[pl.ds(0, 64, stride=2), :]
    up[128:192] = ocean[pl.ds(1, 64, stride=2), :]


def final_kernel(
    atm_mixing, ocean_mixing,
    atm, ocean, operator, below, above, own, in0, in1, in3, in4,
    atm_out, ocean_out,
):
    level = lax.axis_index("lev")
    last = lax.axis_size("lev") - 1
    at_bottom = level == 0
    at_top = level == last
    for field in range(4):
        low, high = atm[field, 0], atm[field, 1]
        rows = slice(16 * field, 16 * field + 16)
        more = slice(64 + 16 * field, 80 + 16 * field)
        beneath = jnp.where(at_bottom, low, jnp.concatenate([below[rows], below[more]], axis=1))
        overhead = jnp.where(at_top, high, jnp.concatenate([above[rows], above[more]], axis=1))
        mixed_low = low + atm_mixing[field, 0] * (high - 2.0 * low + beneath)
        mixed_high = high + atm_mixing[field, 1] * (overhead - 2.0 * high + low)
        mixed = jnp.concatenate([mixed_low, mixed_high], axis=1)
        lateral = jnp.dot(
            operator[...], mixed, precision=lax.Precision.HIGHEST, preferred_element_type=jnp.float32
        )
        result = mixed + 0.25 * lateral
        atm_out[field, 0] = result[:, 0:256]
        atm_out[field, 1] = result[:, 256:512]
    for field in range(2):
        low = ocean[pl.ds(64 * field, 32, stride=2), :]
        high = ocean[pl.ds(64 * field + 1, 32, stride=2), :]
        rows = slice(128 + 32 * field, 160 + 32 * field)
        beneath = jnp.where(at_bottom, low, below[rows])
        overhead = jnp.where(at_top, high, above[rows])
        ocean_out[pl.ds(64 * field, 32, stride=2), :] = low + ocean_mixing[field, 0] * (
            high - 2.0 * low + beneath
        )
        ocean_out[pl.ds(64 * field + 1, 32, stride=2), :] = high + ocean_mixing[field, 1] * (
            overhead - 2.0 * high + low
        )

    @pl.when(at_bottom)
    def _():
        codes = own[4:8]
        for source in range(1, 8):
            codes = codes + own[8 * source + 4 : 8 * source + 8]
        labels = lax.broadcasted_iota(jnp.int32, (64, 64), 0).astype(jnp.float32)
        total = jnp.zeros((64, 128), jnp.float32)
        for reach, inbound in enumerate((in0, in1, own, in3, in4)):
            to = codes[reach // 2 : reach // 2 + 1, 64 * (reach % 2) : 64 * (reach % 2) + 64]
            onehot = (to == labels).astype(jnp.float32).astype(jnp.bfloat16)
            total = total + jnp.dot(
                onehot, inbound[...].astype(jnp.bfloat16), preferred_element_type=jnp.float32
            )
        total = 0.5 * total
        even = ocean_out[pl.ds(0, 32, stride=2), :]
        ocean_out[pl.ds(0, 32, stride=2), :] = even + total[0:32]
        atm_out[2, 0, :, 0:128] = atm_out[2, 0, :, 0:128] + total[32:48]
        atm_out[2, 0, :, 128:256] = atm_out[2, 0, :, 128:256] + total[48:64]


def shards(
    atm_state,
    atm_mixing,
    element_operator,
    ocean_state,
    ocean_mixing,
    atm_flux,
    sea_temp,
    ocean_tiles,
    ocean_tile_src,
    ocean_tile_dst,
    atmos_tiles,
    atmos_tile_src,
    atmos_tile_dst,
):
    columns, levels = lax.axis_size("horiz"), lax.axis_size("lev")
    f32 = jnp.float32
    smem = pl.BlockSpec(memory_space=pltpu.SMEM)
    vmem = pl.BlockSpec(memory_space=pltpu.VMEM)
    ocean_rows = ocean_state.reshape(2, 2, 32, 128).transpose(0, 2, 1, 3).reshape(128, 128)
    send, up, down = pl.pallas_call(
        prep_kernel,
        out_shape=(
            jax.ShapeDtypeStruct((64, 128), f32),
            jax.ShapeDtypeStruct((192, 128), f32),
            jax.ShapeDtypeStruct((192, 128), f32),
        ),
        in_specs=[smem] * 4 + [vmem] * 6,
        out_specs=(vmem, vmem, vmem),
        scratch_shapes=[pltpu.VMEM((64, 128), f32)],
        compiler_params=pltpu.CompilerParams(vmem_limit_bytes=8 << 20),
    )(
        ocean_tile_src, ocean_tile_dst, atmos_tile_src, atmos_tile_dst,
        atm_state, ocean_rows, atm_flux, sea_temp.reshape(32, 128), ocean_tiles, atmos_tiles,
    )
    own = lax.all_to_all(send, "lev", 0, 0, tiled=True)
    own, up, down = lax.optimization_barrier((own, up, down))

    def to_owner(reach):
        step = reach - NEAR
        pairs = [
            (h * levels + LANE[reach], ((h + step) % columns) * levels) for h in range(columns)
        ]
        return lax.ppermute(own, ("horiz", "lev"), pairs)

    inbound = [to_owner(reach) for reach in (0, 1, 3, 4)]
    below = lax.ppermute(up, "lev", [(i, i + 1) for i in range(levels - 1)])
    above = lax.ppermute(down, "lev", [(i + 1, i) for i in range(levels - 1)])
    atm_next, ocean_next = pl.pallas_call(
        final_kernel,
        out_shape=(
            jax.ShapeDtypeStruct(atm_state.shape, f32),
            jax.ShapeDtypeStruct((128, 128), f32),
        ),
        in_specs=[smem] * 2 + [vmem] * 10,
        out_specs=(vmem, vmem),
        compiler_params=pltpu.CompilerParams(vmem_limit_bytes=8 << 20),
    )(
        atm_mixing, ocean_mixing, atm_state, ocean_rows, element_operator,
        below, above, own, *inbound,
    )
    ocean_next = ocean_next.reshape(2, 32, 2, 128).transpose(0, 2, 1, 3).reshape(ocean_state.shape)
    return (atm_next, ocean_next)


def solution(mesh):
    placed = (
        P(None, "lev", None, "horiz"),
        P(None, "lev"),
        P(),
        P(None, "lev", "horiz"),
        P(None, "lev"),
        P(None, "horiz"),
        P("horiz"),
        P(("horiz", "lev"), None, None),
        P(("horiz", "lev")),
        P(("horiz", "lev")),
        P(("horiz", "lev"), None, None),
        P(("horiz", "lev")),
        P(("horiz", "lev")),
    )
    return jax.shard_map(
        shards,
        mesh=mesh,
        in_specs=placed,
        out_specs=(P(None, "lev", None, "horiz"), P(None, "lev", "horiz")),
        check_vma=False,
    )
```

time: 76.5 us -> 55.2 us (0.72)
  the two profiles are of different devices: /device:TPU:32 before, /device:TPU:1 now
where the time goes in v1:
time: 55.2 us; the launch traced here: 54.6 us
  starting transfers between devices  23.2 us (42%)
  blocking collectives  21.4 us (39%)
  local copies, waits for them, and re-layouts  5.86 us (11%)
  Pallas kernels  2.57 us (5%)
  waiting for transfers between devices  0.91 us (2%)
  between operations  0.78 us (1%)
    all_to_all x1, blocking collectives, shards(): own = lax.all_to_all(send, 'lev', 0, 0, tiled=True)  21.4 us
    ppermute x4, starting transfers between devices, to_owner(): return lax.ppermute(own, ('horiz', 'lev'), pairs)  18.3 us
    unnamed x31, local copies, waits for them, and re-layouts  5.86 us
    ppermute x1, starting transfers between devices, shards(): below = lax.ppermute(up, 'lev', [(i, i + 1) for i in range(levels - 1)])  2.94 us
    ppermute x1, starting transfers between devices, shards(): above = lax.ppermute(down, 'lev', [(i + 1, i) for i in range(levels - 1)])  1.92 us
    pallas_call x1, Pallas kernels, shards(): pl.pallas_call(final_kernel, out_shape=(jax.ShapeDtypeStruct(atm_state.sh...  1.56 us
  transfers between devices with their start and end apart: 6, of which 1 were waited for; matrix products, arithmetic and copies ran while one was open for 0% of the time, Pallas kernels for 0%

profile of v1, /device:TPU:1, one launch (start us, length us, event | category | flops | bytes accessed | tf_op | source)
XLA Modules:
  0.0 54.6 jit_solution(17283788619144566059)
XLA Ops:
  0.6 0.0 copy-start.13
  0.6 0.0 copy-start.10
  0.7 0.0 copy-start.11
  0.7 0.6 %copy-done.13 = s32[10]{0:T(128)S(1)} copy-done((s32[10]{0:T(128)S(1)}, s32[10]{0:T(128)}, u32[]{:S(2)}) %copy-start.13) | copy-done | bytes 64
  1.3 0.0 copy-done.10
  1.3 0.0 copy-done.11
  1.3 0.0 copy-done.12
  1.3 0.9 %copy-done = f32[4,2,16,256]{3,2,1,0:T(8,128)S(1)} copy-done((f32[4,2,16,256]{3,2,1,0:T(8,128)S(1)}, f32[4,2,16,256]{3,2,1,0:T(8,128)}, u32[]{:S(2)}) %copy-start) | copy-done | bytes 131096
  2.2 1.0 %copy-done.2 = bf16[10,128,128]{2,1,0:T(8,128)(2,1)S(1)} copy-done((bf16[10,128,128]{2,1,0:T(8,128)(2,1)S(1)}, bf16[10,128,128]{2,1,0:T(8,128)(2,1)}, u32[]{:S(2)}) %copy-start.2) | copy-done | bytes 327704
  3.2 1.0 %copy-done.3 = bf16[10,128,128]{2,1,0:T(8,128)(2,1)S(1)} copy-done((bf16[10,128,128]{2,1,0:T(8,128)(2,1)S(1)}, bf16[10,128,128]{2,1,0:T(8,128)(2,1)}, u32[]{:S(2)}) %copy-start.3) | copy-done | bytes 327704
  4.2 0.8 %copy-done.4 = f32[2,2,4096]{2,1,0:T(2,128)S(1)} copy-done((f32[2,2,4096]{2,1,0:T(2,128)S(1)}, f32[2,2,4096]{2,1,0:T(2,128)}, u32[]{:S(2)}) %copy-start.4) | copy-done | bytes 65560
  5.0 0.7 %copy-done.6 = bf16[16,256]{1,0:T(8,128)(2,1)S(1)} copy-done((bf16[16,256]{1,0:T(8,128)(2,1)S(1)}, bf16[16,256]{1,0:T(8,128)(2,1)}, u32[]{:S(2)}) %copy-start.6) | copy-done | bytes 8216
  5.7 0.7 %copy-done.7 = bf16[4096]{0:T(1024)(128)(2,1)S(1)} copy-done((bf16[4096]{0:T(1024)(128)(2,1)S(1)}, bf16[4096]{0:T(1024)(128)(2,1)}, u32[]{:S(2)}) %copy-start.7) | copy-done | bytes 8216
  6.4 1.0 %shard_map.140 = (f32[64,128]{1,0:T(8,128)S(1)}, f32[192,128]{1,0:T(8,128)S(1)}, f32[192,128]{1,0:T(8,128)S(1)}) custom-call(s32[10]{0:T(128)S(1)} %copy-done.10, s32[10]{0:T(128)S(1)} %copy-done.11, s32[10]{0:T(128)S(1)} %copy-done.12, s32[10]{0:T(128)S(1)} %copy-done.13, f32[4,2,16,256]{3,2,1,0:T(8,128)S(1)} %copy-done, f32[128,128]{1,0:T(8,128)S(1)} %bitcast.13, ...), custom_call_target="tpu_custom_call" | custom-call | tf_op jit(solution)/shard_map/pallas_call | solution.py:142
  7.4 0.0 copy-start.9
  7.5 21.4 %all_to_all.12 = f32[8,8,128]{2,1,0:T(8,128)S(1)} all-to-all(f32[8,8,128]{2,1,0:T(8,128)S(1)} %bitcast.20), channel_id=1, replica_groups=mesh['horiz'=128,'lev'=8] {'lev'}, dimensions={0} | all-to-all | bytes 65536 | tf_op jit(solution)/shard_map/all_to_all | solution.py:157
  28.8 2.9 %collective-permute-start = (f32[192,128]{1,0:T(8,128)S(1)}, f32[192,128]{1,0:T(8,128)S(1)}, u32[]{:S(2)}, u32[]{:S(2)}) collective-permute-start(f32[192,128]{1,0:T(8,128)S(1)} %get-tuple-element.13), channel_id=1, source_target_pairs={{0,1},{1,2},{2,3},{3,4},{4,5},{5,6},{6,7},{8,9},{9,10},{10,11},{11... | collective-permute-start | bytes 294920 | tf_op jit(solution)/shard_map/ppermute | solution.py:168
  31.8 1.9 %collective-permute-start.1 = (f32[192,128]{1,0:T(8,128)S(1)}, f32[192,128]{1,0:T(8,128)S(1)}, u32[]{:S(2)}, u32[]{:S(2)}) collective-permute-start(f32[192,128]{1,0:T(8,128)S(1)} %get-tuple-element.14), channel_id=1, source_target_pairs={{1,0},{2,1},{3,2},{4,3},{5,4},{6,5},{7,6},{9,8},{10,9},{11,10},{12... | collective-permute-start | bytes 294920 | tf_op jit(solution)/shard_map/ppermute | solution.py:169
  33.7 0.7 %collective-permute-start.5 = (f32[64,128]{1,0:T(8,128)S(1)}, f32[64,128]{1,0:T(8,128)S(1)}, u32[]{:S(2)}, u32[]{:S(2)}) collective-permute-start(f32[64,128]{1,0:T(8,128)S(1)} %bitcast.15), channel_id=1, source_target_pairs={{4,16},{12,24},{20,32},{28,40},{36,48},{44,56},{52,64},{60,72},{68... | collective-permute-start | bytes 98312 | tf_op jit(solution)/shard_map/ppermute | solution.py:165
  34.4 0.7 %collective-permute-start.4 = (f32[64,128]{1,0:T(8,128)S(1)}, f32[64,128]{1,0:T(8,128)S(1)}, u32[]{:S(2)}, u32[]{:S(2)}) collective-permute-start(f32[64,128]{1,0:T(8,128)S(1)} %bitcast.16), channel_id=1, source_target_pairs={{3,8},{11,16},{19,24},{27,32},{35,40},{43,48},{51,56},{59,64},{67,... | collective-permute-start | bytes 98312 | tf_op jit(solution)/shard_map/ppermute | solution.py:165
  35.0 0.7 %collective-permute-start.3 = (f32[64,128]{1,0:T(8,128)S(1)}, f32[64,128]{1,0:T(8,128)S(1)}, u32[]{:S(2)}, u32[]{:S(2)}) collective-permute-start(f32[64,128]{1,0:T(8,128)S(1)} %bitcast.17), channel_id=1, source_target_pairs={{2,1016},{10,0},{18,8},{26,16},{34,24},{42,32},{50,40},{58,48},{66... | collective-permute-start | bytes 98312 | tf_op jit(solution)/shard_map/ppermute | solution.py:165
  35.7 0.0 collective-permute-done.5.in4
  35.7 16.3 %collective-permute-start.2 = (f32[64,128]{1,0:T(8,128)S(1)}, f32[64,128]{1,0:T(8,128)S(1)}, u32[]{:S(2)}, u32[]{:S(2)}) collective-permute-start(f32[64,128]{1,0:T(8,128)S(1)} %bitcast.18), channel_id=1, source_target_pairs={{1,1008},{9,1016},{17,0},{25,8},{33,16},{41,24},{49,32},{57,40},{6... | collective-permute-start | bytes 98312 | tf_op jit(solution)/shard_map/ppermute | solution.py:165
  52.0 0.0 copy-done.14
  52.0 0.1 copy.16.atm_mixing
  52.1 0.0 collective-permute-done.4.in3
  52.1 0.0 collective-permute-done.3.in1
  52.1 0.9 %collective-permute-done.2.in0 = f32[64,128]{1,0:T(8,128)S(1)} collective-permute-done((f32[64,128]{1,0:T(8,128)S(1)}, f32[64,128]{1,0:T(8,128)S(1)}, u32[]{:S(2)}, u32[]{:S(2)}) %collective-permute-start.2) | collective-permute-done | bytes 32800 | tf_op jit(solution)/shard_map/ppermute | solution.py:165
  53.0 0.0 collective-permute-done.below
  53.0 0.0 collective-permute-done.1.above
  53.0 0.0 copy-done.1
  53.1 1.6 %shard_map.141 = (f32[4,2,16,256]{3,2,1,0:T(8,128)}, f32[128,128]{1,0:T(8,128)}) custom-call(f32[4,2]{1,0:T(4,128)S(1)} %copy.16.atm_mixing, f32[2,2]{1,0:T(2,128)S(1)} %copy-done.9, f32[4,2,16,256]{3,2,1,0:T(8,128)S(1)} %copy-done.1, f32[128,128]{1,0:T(8,128)S(1)} %bitcast.14, f32[16,16]{1,0:T(8,128)S(1)} %copy-done.8, ...), custom_call_target="tpu_custom_call" | custom-call | tf_op jit(solution)/shard_map/pallas_call | solution.py:170
  (14 shorter events, 0.0 us)
Async XLA Ops:
  0.6 0.7 %copy-start.13 = (s32[10]{0:T(128)S(1)}, s32[10]{0:T(128)}, u32[]{:S(2)}) copy-start(s32[10]{0:T(128)} %atmos_dst.1) | copy-start | bytes 124
  0.6 0.7 %copy-start.10 = (s32[10]{0:T(128)S(1)}, s32[10]{0:T(128)}, u32[]{:S(2)}) copy-start(s32[10]{0:T(128)} %ocean_src.1) | copy-start | bytes 124
  0.7 0.7 %copy-start.11 = (s32[10]{0:T(128)S(1)}, s32[10]{0:T(128)}, u32[]{:S(2)}) copy-start(s32[10]{0:T(128)} %ocean_dst.1) | copy-start | bytes 124
  0.7 0.7 %copy-start.12 = (s32[10]{0:T(128)S(1)}, s32[10]{0:T(128)}, u32[]{:S(2)}) copy-start(s32[10]{0:T(128)} %atmos_src.1) | copy-start | bytes 124
  1.3 0.9 %copy-start = (f32[4,2,16,256]{3,2,1,0:T(8,128)S(1)}, f32[4,2,16,256]{3,2,1,0:T(8,128)}, u32[]{:S(2)}) copy-start(f32[4,2,16,256]{3,2,1,0:T(8,128)} %atm.3) | copy-start | bytes 393220
  2.2 1.0 %copy-start.2 = (bf16[10,128,128]{2,1,0:T(8,128)(2,1)S(1)}, bf16[10,128,128]{2,1,0:T(8,128)(2,1)}, u32[]{:S(2)}) copy-start(bf16[10,128,128]{2,1,0:T(8,128)(2,1)} %ocean_tiles.1) | copy-start | bytes 983044
  3.2 1.0 %copy-start.3 = (bf16[10,128,128]{2,1,0:T(8,128)(2,1)S(1)}, bf16[10,128,128]{2,1,0:T(8,128)(2,1)}, u32[]{:S(2)}) copy-start(bf16[10,128,128]{2,1,0:T(8,128)(2,1)} %atmos_tiles.1) | copy-start | bytes 983044
  4.2 0.8 %copy-start.4 = (f32[2,2,4096]{2,1,0:T(2,128)S(1)}, f32[2,2,4096]{2,1,0:T(2,128)}, u32[]{:S(2)}) copy-start(f32[2,2,4096]{2,1,0:T(2,128)} %param.16) | copy-start | bytes 196612
  5.0 0.7 %copy-start.6 = (bf16[16,256]{1,0:T(8,128)(2,1)S(1)}, bf16[16,256]{1,0:T(8,128)(2,1)}, u32[]{:S(2)}) copy-start(bf16[16,256]{1,0:T(8,128)(2,1)} %flux.1) | copy-start | bytes 24580
  5.7 0.7 %copy-start.7 = (bf16[4096]{0:T(1024)(128)(2,1)S(1)}, bf16[4096]{0:T(1024)(128)(2,1)}, u32[]{:S(2)}) copy-start(bf16[4096]{0:T(1024)(128)(2,1)} %param.19) | copy-start | bytes 24580
  6.4 46.6 %copy-start.1 = (f32[4,2,16,256]{3,2,1,0:T(8,128)S(1)}, f32[4,2,16,256]{3,2,1,0:T(8,128)}, u32[]{:S(2)}) copy-start(f32[4,2,16,256]{3,2,1,0:T(8,128)} %atm.3) | copy-start | bytes 393220
  7.4 45.6 %copy-start.5 = (f32[2,2,4096]{2,1,0:T(2,128)S(1)}, f32[2,2,4096]{2,1,0:T(2,128)}, u32[]{:S(2)}) copy-start(f32[2,2,4096]{2,1,0:T(2,128)} %param.16) | copy-start | bytes 196612
  7.4 44.6 %copy-start.14 = (f32[4,2]{0,1:T(2,128)S(1)}, f32[4,2]{0,1:T(2,128)}, u32[]{:S(2)}) copy-start(f32[4,2]{0,1:T(2,128)} %param.14) | copy-start | bytes 100
  7.4 45.6 %copy-start.9 = (f32[2,2]{1,0:T(2,128)S(1)}, f32[2,2]{1,0:T(2,128)}, u32[]{:S(2)}) copy-start(f32[2,2]{1,0:T(2,128)} %ocean_mixing.1) | copy-start | bytes 52
  28.8 24.3 %copy-start.8 = (f32[16,16]{1,0:T(8,128)S(1)}, f32[16,16]{1,0:T(8,128)}, u32[]{:S(2)}) copy-start(f32[16,16]{1,0:T(8,128)} %operator.1) | copy-start | bytes 3076
  28.8 24.2 %collective-permute-start = (f32[192,128]{1,0:T(8,128)S(1)}, f32[192,128]{1,0:T(8,128)S(1)}, u32[]{:S(2)}, u32[]{:S(2)}) collective-permute-start(f32[192,128]{1,0:T(8,128)S(1)} %get-tuple-element.13), channel_id=1, source_target_pairs={{0,1},{1,2},{2,3},{3,4},{4,5},{5,6},{6,7},{8,9},{9,10},{10,11},{11... | collective-permute-start | bytes 294920 | tf_op jit(solution)/shard_map/ppermute | solution.py:168
  31.8 21.3 %collective-permute-start.1 = (f32[192,128]{1,0:T(8,128)S(1)}, f32[192,128]{1,0:T(8,128)S(1)}, u32[]{:S(2)}, u32[]{:S(2)}) collective-permute-start(f32[192,128]{1,0:T(8,128)S(1)} %get-tuple-element.14), channel_id=1, source_target_pairs={{1,0},{2,1},{3,2},{4,3},{5,4},{6,5},{7,6},{9,8},{10,9},{11,10},{12... | collective-permute-start | bytes 294920 | tf_op jit(solution)/shard_map/ppermute | solution.py:169
  33.7 2.0 %collective-permute-start.5 = (f32[64,128]{1,0:T(8,128)S(1)}, f32[64,128]{1,0:T(8,128)S(1)}, u32[]{:S(2)}, u32[]{:S(2)}) collective-permute-start(f32[64,128]{1,0:T(8,128)S(1)} %bitcast.15), channel_id=1, source_target_pairs={{4,16},{12,24},{20,32},{28,40},{36,48},{44,56},{52,64},{60,72},{68... | collective-permute-start | bytes 98312 | tf_op jit(solution)/shard_map/ppermute | solution.py:165
  34.4 17.8 %collective-permute-start.4 = (f32[64,128]{1,0:T(8,128)S(1)}, f32[64,128]{1,0:T(8,128)S(1)}, u32[]{:S(2)}, u32[]{:S(2)}) collective-permute-start(f32[64,128]{1,0:T(8,128)S(1)} %bitcast.16), channel_id=1, source_target_pairs={{3,8},{11,16},{19,24},{27,32},{35,40},{43,48},{51,56},{59,64},{67,... | collective-permute-start | bytes 98312 | tf_op jit(solution)/shard_map/ppermute | solution.py:165
  35.0 17.1 %collective-permute-start.3 = (f32[64,128]{1,0:T(8,128)S(1)}, f32[64,128]{1,0:T(8,128)S(1)}, u32[]{:S(2)}, u32[]{:S(2)}) collective-permute-start(f32[64,128]{1,0:T(8,128)S(1)} %bitcast.17), channel_id=1, source_target_pairs={{2,1016},{10,0},{18,8},{26,16},{34,24},{42,32},{50,40},{58,48},{66... | collective-permute-start | bytes 98312 | tf_op jit(solution)/shard_map/ppermute | solution.py:165
  35.7 17.3 %collective-permute-start.2 = (f32[64,128]{1,0:T(8,128)S(1)}, f32[64,128]{1,0:T(8,128)S(1)}, u32[]{:S(2)}, u32[]{:S(2)}) collective-permute-start(f32[64,128]{1,0:T(8,128)S(1)} %bitcast.18), channel_id=1, source_target_pairs={{1,1008},{9,1016},{17,0},{25,8},{33,16},{41,24},{49,32},{57,40},{6... | collective-permute-start | bytes 98312 | tf_op jit(solution)/shard_map/ppermute | solution.py:165

commit v2 on v0

v2 whole, which is shorter than its diff:
```python
import jax
import jax.numpy as jnp
from jax import lax
from jax.experimental import pallas as pl
from jax.experimental.pallas import tpu as pltpu
from jax.sharding import PartitionSpec as P

BLOCK = 128
NEAR = 2
CAP = 2
REACH = 2 * NEAR + 1
NEXT = ((0, 2), (0, 1))
PREVIOUS = ((1, 6), (1, 1))
EMPTY = 64


def prep_kernel(
    ocean_src_hbm, ocean_dst_hbm, atmos_src_hbm, atmos_dst_hbm,
    atm_hbm, ocean_hbm, flux_hbm, sea_hbm, ocean_tiles_hbm, atmos_tiles_hbm,
    send, up, down,
    ocean_src, ocean_dst, atmos_src, atmos_dst, ocean, flux, sea, ocean_tiles, atmos_tiles, picks, rows_out, sems,
):
    level = lax.axis_index("lev")
    odd = lax.axis_index("horiz") % 2
    moves = [
        (flux_hbm, flux), (sea_hbm, sea), (ocean_src_hbm, ocean_src), (atmos_src_hbm, atmos_src),
        (ocean_dst_hbm, ocean_dst), (atmos_dst_hbm, atmos_dst),
        (ocean_tiles_hbm, ocean_tiles), (atmos_tiles_hbm, atmos_tiles),
        (ocean_hbm, ocean),
        (atm_hbm.at[:, 1, :, 0:128], up.at[0:4]), (atm_hbm.at[:, 1, :, 128:256], up.at[4:8]),
        (atm_hbm.at[:, 0, :, 0:128], down.at[0:4]), (atm_hbm.at[:, 0, :, 128:256], down.at[4:8]),
    ]
    copies = [
        pltpu.make_async_copy(source, target, sems.at[i]) for i, (source, target) in enumerate(moves)
    ]
    for copy in copies:
        copy.start()
    rows_out[...] = jnp.zeros_like(rows_out)
    for copy in copies[0:6]:
        copy.wait()
    lane = lax.broadcasted_iota(jnp.int32, (4, 128), 1)
    line = lax.broadcasted_iota(jnp.int32, (4, 128), 0)
    inside = lane % 64 - 8 * level
    codes = jnp.where((inside >= 0) & (inside < 8), EMPTY, 0)
    for reach in range(REACH):
        delta = reach - NEAR
        array_even, from_even = (0, -delta) if -delta in (0, 1) else (1, 2 - delta) if delta > 0 else (2, -delta - 2)
        array_odd, from_odd = (0, 1 - delta) if 1 - delta in (0, 1) else (1, 3 - delta) if delta > 0 else (2, -delta - 1)
        here = (line == jnp.where(odd == 0, array_even, array_odd)) & (
            lane // 64 == jnp.where(odd == 0, from_even, from_odd)
        )
        for place in range(CAP):
            to = ocean_dst[reach * CAP + place]
            codes = jnp.where(here & (inside == place), jnp.where(to < 32, to, EMPTY), codes)
            to = atmos_dst[reach * CAP + place]
            code = jnp.where(to < 32, 32 + (to % 2) * 16 + to // 2, EMPTY)
            codes = jnp.where(here & (inside == CAP + place), code, codes)
    rows_out[pl.ds(64 * odd + 4, 4), :] = codes.astype(jnp.float32)
    picks[0:16] = flux[:, 0:128].astype(jnp.float32)
    picks[16:32] = flux[:, 128:256].astype(jnp.float32)
    picks[32:64] = sea[...].astype(jnp.float32)

    def product(row, tile):
        return lax.dot_general(
            row.astype(jnp.bfloat16), tile, (((1,), (1,)), ((), ())), preferred_element_type=jnp.float32
        ).astype(jnp.bfloat16).astype(jnp.float32)

    def chunk(reach):
        def member(target):
            column, lev = PREVIOUS[target + 2] if target < 0 else NEXT[target - 2] if target > 1 else (target, 0)
            return column * 8 + lev

        return 8 * jnp.where(odd == 0, member(reach - NEAR), member(reach - NEAR + 1))

    copies[6].wait()
    for slot in range(REACH * CAP):
        source = ocean_src[slot]
        row = picks[pl.ds((source % 2) * 16 + source // 2, 1), :]
        rows_out[pl.ds(chunk(slot // CAP) + slot % CAP, 1), :] = product(row, ocean_tiles[slot])
    copies[7].wait()
    for slot in range(REACH * CAP):
        row = picks[pl.ds(32 + atmos_src[slot], 1), :]
        rows_out[pl.ds(chunk(slot // CAP) + CAP + slot % CAP, 1), :] = product(row, atmos_tiles[slot])
    send[...] = rows_out[...].astype(jnp.bfloat16)
    copies[8].wait()
    down[8:12] = ocean[pl.ds(0, 64, stride=2), :].reshape(4, 16, 128)
    up[8:12] = ocean[pl.ds(1, 64, stride=2), :].reshape(4, 16, 128)
    for copy in copies[9:]:
        copy.wait()


def column_kernel(
    atm_mixing, ocean_mixing, atm, ocean, operator, below, above,
    atm_hbm, ocean_hbm, atm_base, ocean_base,
    atm_out, ocean_out, sems,
):
    level = lax.axis_index("lev")
    at_bottom = level == 0
    at_top = level == lax.axis_size("lev") - 1
    for field in range(2):
        low = ocean[pl.ds(64 * field, 32, stride=2), :]
        high = ocean[pl.ds(64 * field + 1, 32, stride=2), :]
        beneath = jnp.where(at_bottom, low, below[8 + 2 * field : 10 + 2 * field].reshape(32, 128))
        overhead = jnp.where(at_top, high, above[8 + 2 * field : 10 + 2 * field].reshape(32, 128))
        ocean_out[pl.ds(64 * field, 32, stride=2), :] = low + ocean_mixing[field, 0] * (
            high - 2.0 * low + beneath
        )
        ocean_out[pl.ds(64 * field + 1, 32, stride=2), :] = high + ocean_mixing[field, 1] * (
            overhead - 2.0 * high + low
        )
    ocean_copy = pltpu.make_async_copy(ocean_out, ocean_hbm, sems.at[0])
    ocean_copy.start()
    ocean_base[...] = ocean_out[0:64]
    for field in range(4):
        low, high = atm[field, 0], atm[field, 1]
        beneath = jnp.where(at_bottom, low, jnp.concatenate([below[field], below[4 + field]], axis=1))
        overhead = jnp.where(at_top, high, jnp.concatenate([above[field], above[4 + field]], axis=1))
        mixed_low = low + atm_mixing[0, field] * (high - 2.0 * low + beneath)
        mixed_high = high + atm_mixing[1, field] * (overhead - 2.0 * high + low)
        mixed = jnp.concatenate([mixed_low, mixed_high], axis=1)
        lateral = jnp.dot(
            operator[...], mixed, precision=lax.Precision.HIGHEST, preferred_element_type=jnp.float32
        )
        result = mixed + 0.25 * lateral
        atm_out[field, 0] = result[:, 0:256]
        atm_out[field, 1] = result[:, 256:512]
    atm_copy = pltpu.make_async_copy(atm_out, atm_hbm, sems.at[1])
    atm_copy.start()
    atm_base[...] = atm_out[2, 0]
    ocean_copy.wait()
    atm_copy.wait()


def surface_kernel(
    atm_in, ocean_in, atm_base, ocean_base, own, previous, following,
    atm_hbm, ocean_hbm,
    atm_rows, ocean_rows, sems,
):
    del atm_in, ocean_in

    @pl.when(lax.axis_index("lev") == 0)
    def _():
        codes = jnp.sum(own[...].astype(jnp.float32).reshape(16, 8, 128), axis=0)
        labels = lax.broadcasted_iota(jnp.int32, (64, 128), 0).astype(jnp.float32)
        total = jnp.zeros((64, 128), jnp.float32)
        for i, inbound in enumerate((own, previous, following)):
            onehot = jnp.where(codes[4 + i : 5 + i] == labels, 1.0, 0.0).astype(jnp.bfloat16)
            total = total + jnp.dot(onehot, inbound[...], preferred_element_type=jnp.float32)
        total = 0.5 * total
        ocean_rows[...] = ocean_base[...]
        ocean_rows[pl.ds(0, 32, stride=2), :] = ocean_base[pl.ds(0, 32, stride=2), :] + total[0:32]
        ocean_copy = pltpu.make_async_copy(ocean_rows, ocean_hbm.at[0:64], sems.at[0])
        ocean_copy.start()
        atm_rows[:, 0:128] = atm_base[:, 0:128] + total[32:48]
        atm_rows[:, 128:256] = atm_base[:, 128:256] + total[48:64]
        atm_copy = pltpu.make_async_copy(atm_rows, atm_hbm.at[2, 0], sems.at[1])
        atm_copy.start()
        ocean_copy.wait()
        atm_copy.wait()


def shards(
    atm_state,
    atm_mixing,
    element_operator,
    ocean_state,
    ocean_mixing,
    atm_flux,
    sea_temp,
    ocean_tiles,
    ocean_tile_src,
    ocean_tile_dst,
    atmos_tiles,
    atmos_tile_src,
    atmos_tile_dst,
):
    columns, levels = lax.axis_size("horiz"), lax.axis_size("lev")
    f32, bf16 = jnp.float32, jnp.bfloat16
    vmem = pl.BlockSpec(memory_space=pltpu.VMEM)
    hbm = pl.BlockSpec(memory_space=pltpu.HBM)
    smem = pl.BlockSpec(memory_space=pltpu.SMEM)
    shape = jax.ShapeDtypeStruct
    params = pltpu.CompilerParams(vmem_limit_bytes=8 << 20)
    whole = pltpu.CompilerParams(vmem_limit_bytes=61 << 20)
    ocean_rows = ocean_state.reshape(2, 2, 32, 128).transpose(0, 2, 1, 3).reshape(128, 128)
    send, up, down = pl.pallas_call(
        prep_kernel,
        out_shape=(
            shape((128, 128), bf16),
            shape((12, 16, 128), f32),
            shape((12, 16, 128), f32),
        ),
        in_specs=[hbm] * 10,
        out_specs=(vmem,) * 3,
        scratch_shapes=[pltpu.SMEM((REACH * CAP,), jnp.int32)] * 4
        + [
            pltpu.VMEM((128, 128), f32),
            pltpu.VMEM((16, 256), bf16),
            pltpu.VMEM((32, 128), bf16),
            pltpu.VMEM((REACH * CAP, BLOCK, BLOCK), bf16),
            pltpu.VMEM((REACH * CAP, BLOCK, BLOCK), bf16),
            pltpu.VMEM((64, 128), f32),
            pltpu.VMEM((128, 128), f32),
            pltpu.SemaphoreType.DMA((13,)),
        ],
        compiler_params=whole,
    )(
        ocean_tile_src, ocean_tile_dst, atmos_tile_src, atmos_tile_dst,
        atm_state, ocean_rows, atm_flux, sea_temp.reshape(32, 128), ocean_tiles, atmos_tiles,
    )
    pairs = [[h * levels + l for h in (g, g + 1) for l in range(levels)] for g in range(0, columns, 2)]
    own = lax.all_to_all(send, ("horiz", "lev"), 0, 0, axis_index_groups=pairs, tiled=True)

    def to_owner(lanes, step):
        return lax.ppermute(
            own,
            ("horiz", "lev"),
            [
                ((g + column) * levels + lev, (g + step + i) % columns * levels)
                for g in range(0, columns, 2)
                for i, (column, lev) in enumerate(lanes)
            ],
        )

    previous = to_owner(NEXT, 2)
    following = to_owner(PREVIOUS, -2)
    below = lax.ppermute(up, "lev", [(i, i + 1) for i in range(levels - 1)])
    above = lax.ppermute(down, "lev", [(i + 1, i) for i in range(levels - 1)])
    atm_next, ocean_next, atm_base, ocean_base = pl.pallas_call(
        column_kernel,
        out_shape=(
            shape(atm_state.shape, f32),
            shape((128, 128), f32),
            shape((16, 256), f32),
            shape((64, 128), f32),
        ),
        in_specs=[smem] * 2 + [vmem] * 5,
        out_specs=(hbm, hbm, vmem, vmem),
        scratch_shapes=[
            pltpu.VMEM(atm_state.shape, f32),
            pltpu.VMEM((128, 128), f32),
            pltpu.SemaphoreType.DMA((2,)),
        ],
        compiler_params=params,
    )(atm_mixing.T, ocean_mixing, atm_state, ocean_rows, element_operator, below, above)
    atm_next, ocean_next = pl.pallas_call(
        surface_kernel,
        out_shape=(shape(atm_state.shape, f32), shape((128, 128), f32)),
        in_specs=[hbm] * 2 + [vmem] * 5,
        out_specs=(hbm, hbm),
        scratch_shapes=[
            pltpu.VMEM((16, 256), f32),
            pltpu.VMEM((64, 128), f32),
            pltpu.SemaphoreType.DMA((2,)),
        ],
        input_output_aliases={0: 0, 1: 1},
        compiler_params=params,
    )(atm_next, ocean_next, atm_base, ocean_base, own, previous, following)
    ocean_next = ocean_next.reshape(2, 32, 2, 128).transpose(0, 2, 1, 3).reshape(ocean_state.shape)
    return (atm_next, ocean_next)


def solution(mesh):
    placed = (
        P(None, "lev", None, "horiz"),
        P(None, "lev"),
        P(),
        P(None, "lev", "horiz"),
        P(None, "lev"),
        P(None, "horiz"),
        P("horiz"),
        P(("horiz", "lev"), None, None),
        P(("horiz", "lev")),
        P(("horiz", "lev")),
        P(("horiz", "lev"), None, None),
        P(("horiz", "lev")),
        P(("horiz", "lev")),
    )
    return jax.shard_map(
        shards,
        mesh=mesh,
        in_specs=placed,
        out_specs=(P(None, "lev", None, "horiz"), P(None, "lev", "horiz")),
        check_vma=False,
    )
```

time: 76.5 us -> 38 us (0.50)
  the two profiles are of different devices: /device:TPU:32 before, /device:TPU:38 now
where the time goes in v2:
time: 38 us; the launch traced here: 37.7 us
  starting transfers between devices  32.9 us (87%)
  Pallas kernels  3.99 us (10%)
  between operations  0.8 us (2%)
    all_to_all x1, starting transfers between devices, shards(): lax.all_to_all(send, ('horiz', 'lev'), 0, 0, axis_index_groups=pairs, til...  16.2 us
    ppermute x2, starting transfers between devices, to_owner(): lax.ppermute(own, ('horiz', 'lev'), [((g + column) * levels + lev, (g + s...  11.1 us
    ppermute x1, starting transfers between devices, shards(): above = lax.ppermute(down, 'lev', [(i + 1, i) for i in range(levels - 1)])  3.5 us
    pallas_call x1, Pallas kernels, shards(): pl.pallas_call(prep_kernel, out_shape=(shape((128, 128), bf16), shape((12...  2.42 us
    ppermute x1, starting transfers between devices, shards(): below = lax.ppermute(up, 'lev', [(i, i + 1) for i in range(levels - 1)])  2.04 us
    pallas_call x1, Pallas kernels, shards(): pl.pallas_call(column_kernel, out_shape=(shape(atm_state.shape, f32), sha...  1.54 us
  transfers between devices with their start and end apart: 5, of which 0 were waited for; matrix products, arithmetic and copies ran while one was open for 0% of the time, Pallas kernels for 4%

profile of v2, /device:TPU:38, one launch (start us, length us, event | category | flops | bytes accessed | tf_op | source)
XLA Modules:
  0.0 37.7 jit_solution(2910500559807761456)
XLA Ops:
  0.6 0.0 copy-start
  0.6 2.4 %shard_map.140 = (bf16[128,128]{1,0:T(8,128)(2,1)}, f32[12,16,128]{2,1,0:T(8,128)}, f32[12,16,128]{2,1,0:T(8,128)}) custom-call(s32[10]{0:T(128)} %ocean_src_hbm.1, s32[10]{0:T(128)} %ocean_dst_hbm.1, s32[10]{0:T(128)} %atmos_src_hbm.1, s32[10]{0:T(128)} %atmos_dst_hbm.1, f32[4,2,16,256]{3,2,1,0:T(8,128)} %atm.1, f32[128,128]{1,0:T(8,128)} %bitcast.14, ...), custom_call_target="tpu_custom_call" | custom-call | tf_op jit(solution)/shard_map/pallas_call | solution.py:186
  3.1 0.0 copy-start.1
  3.1 0.0 copy-start.2
  3.1 16.2 %all-to-all-start = ((bf16[16,8,128]{2,1,0:T(8,128)(2,1)}), bf16[16,8,128]{2,1,0:T(8,128)(2,1)S(1)}, u32[]{:S(2)}, u32[]{:S(2)}) async-start(bf16[16,8,128]{2,1,0:T(8,128)(2,1)} %bitcast.21), calls=%async_computation | async-start | bytes 65536 | tf_op jit(solution)/shard_map/all_to_all | solution.py:212
  19.3 2.0 %collective-permute-start = (f32[12,16,128]{2,1,0:T(8,128)}, f32[12,16,128]{2,1,0:T(8,128)S(1)}, u32[]{:S(2)}, u32[]{:S(2)}) collective-permute-start(f32[12,16,128]{2,1,0:T(8,128)} %get-tuple-element.11), channel_id=1, source_target_pairs={{0,1},{1,2},{2,3},{3,4},{4,5},{5,6},{6,7},{8,9},{9,10},{10,11},{11... | collective-permute-start | bytes 294920 | tf_op jit(solution)/shard_map/ppermute | solution.py:227
  21.3 3.5 %collective-permute-start.1 = (f32[12,16,128]{2,1,0:T(8,128)}, f32[12,16,128]{2,1,0:T(8,128)S(1)}, u32[]{:S(2)}, u32[]{:S(2)}) collective-permute-start(f32[12,16,128]{2,1,0:T(8,128)} %get-tuple-element.12), channel_id=1, source_target_pairs={{1,0},{2,1},{3,2},{4,3},{5,4},{6,5},{7,6},{9,8},{10,9},{11,10},{12... | collective-permute-start | bytes 294920 | tf_op jit(solution)/shard_map/ppermute | solution.py:228
  24.9 0.0 all-to-all-done
  24.9 0.0 copy-start.4
  24.9 0.0 copy-start.3
  24.9 10.5 %collective-permute-start.3 = (bf16[128,128]{1,0:T(8,128)(2,1)S(1)}, bf16[128,128]{1,0:T(8,128)(2,1)S(1)}, u32[]{:S(2)}, u32[]{:S(2)}) collective-permute-start(bf16[128,128]{1,0:T(8,128)(2,1)S(1)} %bitcast.16), channel_id=1, source_target_pairs={{14,1008},{9,1016},{30,0},{25,8},{46,16},{41,24},{62,32},{57,40},{... | collective-permute-start | bytes 98312 | tf_op jit(solution)/shard_map/ppermute | solution.py:215
  35.4 0.7 %collective-permute-start.2 = (bf16[128,128]{1,0:T(8,128)(2,1)S(1)}, bf16[128,128]{1,0:T(8,128)(2,1)S(1)}, u32[]{:S(2)}, u32[]{:S(2)}) collective-permute-start(bf16[128,128]{1,0:T(8,128)(2,1)S(1)} %bitcast.17), channel_id=1, source_target_pairs={{2,16},{1,24},{18,32},{17,40},{34,48},{33,56},{50,64},{49,72},{66,... | collective-permute-start | bytes 98312 | tf_op jit(solution)/shard_map/ppermute | solution.py:215
  36.0 0.0 collective-permute-done.below
  36.0 0.0 collective-permute-done.1.above
  36.1 0.0 copy-done
  36.1 0.0 copy-done.1
  36.1 0.0 copy-done.2
  36.1 0.0 copy-done.4
  36.1 0.0 copy-done.3
  36.1 1.5 %shard_map.141 = (f32[4,2,16,256]{3,2,1,0:T(8,128)}, f32[128,128]{1,0:T(8,128)}, f32[16,256]{1,0:T(8,128)S(1)}, f32[64,128]{1,0:T(8,128)S(1)}) custom-call(f32[2,4]{1,0:T(2,128)S(1)} %bitcast.19, f32[2,2]{1,0:T(2,128)S(1)} %copy-done.4, f32[4,2,16,256]{3,2,1,0:T(8,128)S(1)} %copy-done, f32[128,128]{1,0:T(8,128)S(1)} %bitcast.15, f32[16,16]{1,0:T(8,128)S(1)} %copy-done.2, ...), custom_call_target="tpu_custom_call" | custom-call | tf_op jit(solution)/shard_map/pallas_call | solution.py:229
  37.6 0.0 collective-permute-done.3.following
  37.7 0.0 collective-permute-done.2.previous
  (1 shorter events, 0.0 us)
Async XLA Ops:
  0.6 35.4 %copy-start = (f32[4,2,16,256]{3,2,1,0:T(8,128)S(1)}, f32[4,2,16,256]{3,2,1,0:T(8,128)}, u32[]{:S(2)}) copy-start(f32[4,2,16,256]{3,2,1,0:T(8,128)} %atm.1) | copy-start | bytes 393220
  3.1 33.0 %copy-start.1 = (f32[2,2,4096]{2,1,0:T(2,128)S(1)}, f32[2,2,4096]{2,1,0:T(2,128)}, u32[]{:S(2)}) copy-start(f32[2,2,4096]{2,1,0:T(2,128)} %param.16) | copy-start | bytes 196612
  3.1 33.0 %copy-start.2 = (f32[16,16]{1,0:T(8,128)S(1)}, f32[16,16]{1,0:T(8,128)}, u32[]{:S(2)}) copy-start(f32[16,16]{1,0:T(8,128)} %operator.1) | copy-start | bytes 3076
  3.1 21.8 %all-to-all-start = ((bf16[16,8,128]{2,1,0:T(8,128)(2,1)}), bf16[16,8,128]{2,1,0:T(8,128)(2,1)S(1)}, u32[]{:S(2)}, u32[]{:S(2)}) async-start(bf16[16,8,128]{2,1,0:T(8,128)(2,1)} %bitcast.21), calls=%async_computation | async-start | bytes 65536 | tf_op jit(solution)/shard_map/all_to_all | solution.py:212
  19.3 16.8 %collective-permute-start = (f32[12,16,128]{2,1,0:T(8,128)}, f32[12,16,128]{2,1,0:T(8,128)S(1)}, u32[]{:S(2)}, u32[]{:S(2)}) collective-permute-start(f32[12,16,128]{2,1,0:T(8,128)} %get-tuple-element.11), channel_id=1, source_target_pairs={{0,1},{1,2},{2,3},{3,4},{4,5},{5,6},{6,7},{8,9},{9,10},{10,11},{11... | collective-permute-start | bytes 294920 | tf_op jit(solution)/shard_map/ppermute | solution.py:227
  21.3 14.7 %collective-permute-start.1 = (f32[12,16,128]{2,1,0:T(8,128)}, f32[12,16,128]{2,1,0:T(8,128)S(1)}, u32[]{:S(2)}, u32[]{:S(2)}) collective-permute-start(f32[12,16,128]{2,1,0:T(8,128)} %get-tuple-element.12), channel_id=1, source_target_pairs={{1,0},{2,1},{3,2},{4,3},{5,4},{6,5},{7,6},{9,8},{10,9},{11,10},{12... | collective-permute-start | bytes 294920 | tf_op jit(solution)/shard_map/ppermute | solution.py:228
  24.9 11.2 %copy-start.4 = (f32[2,2]{1,0:T(2,128)S(1)}, f32[2,2]{1,0:T(2,128)}, u32[]{:S(2)}) copy-start(f32[2,2]{1,0:T(2,128)} %ocean_mixing.1) | copy-start | bytes 52
  24.9 11.2 %copy-start.3 = (f32[4,2]{0,1:T(2,128)S(1)}, f32[4,2]{0,1:T(2,128)}, u32[]{:S(2)}) copy-start(f32[4,2]{0,1:T(2,128)} %param.14) | copy-start | bytes 100
  24.9 12.8 %collective-permute-start.3 = (bf16[128,128]{1,0:T(8,128)(2,1)S(1)}, bf16[128,128]{1,0:T(8,128)(2,1)S(1)}, u32[]{:S(2)}, u32[]{:S(2)}) collective-permute-start(bf16[128,128]{1,0:T(8,128)(2,1)S(1)} %bitcast.16), channel_id=1, source_target_pairs={{14,1008},{9,1016},{30,0},{25,8},{46,16},{41,24},{62,32},{57,40},{... | collective-permute-start | bytes 98312 | tf_op jit(solution)/shard_map/ppermute | solution.py:215
  35.4 2.3 %collective-permute-start.2 = (bf16[128,128]{1,0:T(8,128)(2,1)S(1)}, bf16[128,128]{1,0:T(8,128)(2,1)S(1)}, u32[]{:S(2)}, u32[]{:S(2)}) collective-permute-start(bf16[128,128]{1,0:T(8,128)(2,1)S(1)} %bitcast.17), channel_id=1, source_target_pairs={{2,16},{1,24},{18,32},{17,40},{34,48},{33,56},{50,64},{49,72},{66,... | collective-permute-start | bytes 98312 | tf_op jit(solution)/shard_map/ppermute | solution.py:215

commit v3 on v2

--- a/solution.py
+++ b/solution.py
@@ -9,8 +9,8 @@
 NEAR = 2
 CAP = 2
 REACH = 2 * NEAR + 1
-NEXT = ((0, 2), (0, 1))
-PREVIOUS = ((1, 6), (1, 1))
+NEXT = ((0, 1), (1, 1))
+PREVIOUS = ((1, 6), (1, 2))
 EMPTY = 64
 
 
@@ -22,6 +22,7 @@
 ):
     level = lax.axis_index("lev")
     odd = lax.axis_index("horiz") % 2
+    odd_pair = lax.axis_index("horiz") // 2 % 2
     moves = [
         (flux_hbm, flux), (sea_hbm, sea), (ocean_src_hbm, ocean_src), (atmos_src_hbm, atmos_src),
         (ocean_dst_hbm, ocean_dst), (atmos_dst_hbm, atmos_dst),
@@ -46,7 +47,8 @@
         delta = reach - NEAR
         array_even, from_even = (0, -delta) if -delta in (0, 1) else (1, 2 - delta) if delta > 0 else (2, -delta - 2)
         array_odd, from_odd = (0, 1 - delta) if 1 - delta in (0, 1) else (1, 3 - delta) if delta > 0 else (2, -delta - 1)
-        here = (line == jnp.where(odd == 0, array_even, array_odd)) & (
+        array = jnp.where(odd == 0, array_even, array_odd)
+        here = (line == jnp.where((odd_pair == 1) & (array > 0), 3 - array, array)) & (
             lane // 64 == jnp.where(odd == 0, from_even, from_odd)
         )
         for place in range(CAP):
@@ -72,6 +74,9 @@
 
         return 8 * jnp.where(odd == 0, member(reach - NEAR), member(reach - NEAR + 1))
 
+    copies[8].wait()
+    down[8:12] = ocean[pl.ds(0, 64, stride=2), :].reshape(4, 16, 128)
+    up[8:12] = ocean[pl.ds(1, 64, stride=2), :].reshape(4, 16, 128)
     copies[6].wait()
     for slot in range(REACH * CAP):
         source = ocean_src[slot]
@@ -82,9 +87,6 @@
         row = picks[pl.ds(32 + atmos_src[slot], 1), :]
         rows_out[pl.ds(chunk(slot // CAP) + CAP + slot % CAP, 1), :] = product(row, atmos_tiles[slot])
     send[...] = rows_out[...].astype(jnp.bfloat16)
-    copies[8].wait()
-    down[8:12] = ocean[pl.ds(0, 64, stride=2), :].reshape(4, 16, 128)
-    up[8:12] = ocean[pl.ds(1, 64, stride=2), :].reshape(4, 16, 128)
     for copy in copies[9:]:
         copy.wait()
 
@@ -102,10 +104,10 @@
         high = ocean[pl.ds(64 * field + 1, 32, stride=2), :]
         beneath = jnp.where(at_bottom, low, below[8 + 2 * field : 10 + 2 * field].reshape(32, 128))
         overhead = jnp.where(at_top, high, above[8 + 2 * field : 10 + 2 * field].reshape(32, 128))
-        ocean_out[pl.ds(64 * field, 32, stride=2), :] = low + ocean_mixing[field, 0] * (
+        ocean_out[pl.ds(64 * field, 32, stride=2), :] = low + ocean_mixing[field : field + 1, 0:1] * (
             high - 2.0 * low + beneath
         )
-        ocean_out[pl.ds(64 * field + 1, 32, stride=2), :] = high + ocean_mixing[field, 1] * (
+        ocean_out[pl.ds(64 * field + 1, 32, stride=2), :] = high + ocean_mixing[field : field + 1, 1:2] * (
             overhead - 2.0 * high + low
         )
     ocean_copy = pltpu.make_async_copy(ocean_out, ocean_hbm, sems.at[0])
@@ -115,8 +117,8 @@
         low, high = atm[field, 0], atm[field, 1]
         beneath = jnp.where(at_bottom, low, jnp.concatenate([below[field], below[4 + field]], axis=1))
         overhead = jnp.where(at_top, high, jnp.concatenate([above[field], above[4 + field]], axis=1))
-        mixed_low = low + atm_mixing[0, field] * (high - 2.0 * low + beneath)
-        mixed_high = high + atm_mixing[1, field] * (overhead - 2.0 * high + low)
+        mixed_low = low + atm_mixing[0:1, field : field + 1] * (high - 2.0 * low + beneath)
+        mixed_high = high + atm_mixing[1:2, field : field + 1] * (overhead - 2.0 * high + low)
         mixed = jnp.concatenate([mixed_low, mixed_high], axis=1)
         lateral = jnp.dot(
             operator[...], mixed, precision=lax.Precision.HIGHEST, preferred_element_type=jnp.float32
@@ -132,7 +134,7 @@
 
 
 def surface_kernel(
-    atm_in, ocean_in, atm_base, ocean_base, own, previous, following,
+    atm_in, ocean_in, atm_base, ocean_base, own, second, first,
     atm_hbm, ocean_hbm,
     atm_rows, ocean_rows, sems,
 ):
@@ -143,7 +145,7 @@
         codes = jnp.sum(own[...].astype(jnp.float32).reshape(16, 8, 128), axis=0)
         labels = lax.broadcasted_iota(jnp.int32, (64, 128), 0).astype(jnp.float32)
         total = jnp.zeros((64, 128), jnp.float32)
-        for i, inbound in enumerate((own, previous, following)):
+        for i, inbound in enumerate((own, first, second)):
             onehot = jnp.where(codes[4 + i : 5 + i] == labels, 1.0, 0.0).astype(jnp.bfloat16)
             total = total + jnp.dot(onehot, inbound[...], preferred_element_type=jnp.float32)
         total = 0.5 * total
@@ -178,7 +180,6 @@
     f32, bf16 = jnp.float32, jnp.bfloat16
     vmem = pl.BlockSpec(memory_space=pltpu.VMEM)
     hbm = pl.BlockSpec(memory_space=pltpu.HBM)
-    smem = pl.BlockSpec(memory_space=pltpu.SMEM)
     shape = jax.ShapeDtypeStruct
     params = pltpu.CompilerParams(vmem_limit_bytes=8 << 20)
     whole = pltpu.CompilerParams(vmem_limit_bytes=61 << 20)
@@ -211,19 +212,18 @@
     pairs = [[h * levels + l for h in (g, g + 1) for l in range(levels)] for g in range(0, columns, 2)]
     own = lax.all_to_all(send, ("horiz", "lev"), 0, 0, axis_index_groups=pairs, tiled=True)
 
-    def to_owner(lanes, step):
-        return lax.ppermute(
-            own,
-            ("horiz", "lev"),
-            [
-                ((g + column) * levels + lev, (g + step + i) % columns * levels)
-                for g in range(0, columns, 2)
-                for i, (column, lev) in enumerate(lanes)
-            ],
-        )
-
-    previous = to_owner(NEXT, 2)
-    following = to_owner(PREVIOUS, -2)
+    def swap(wave):
+        pairs = []
+        for g in range(2 - 2 * wave, columns, 4):
+            for i in range(2):
+                column, lev = NEXT[i]
+                pairs.append(((g + column) * levels + lev, (g + 2 + i) % columns * levels))
+                column, lev = PREVIOUS[i]
+                pairs.append((((g + 2) % columns + column) * levels + lev, (g + i) * levels))
+        return lax.ppermute(own, ("horiz", "lev"), pairs)
+
+    second = swap(1)
+    first = swap(0)
     below = lax.ppermute(up, "lev", [(i, i + 1) for i in range(levels - 1)])
     above = lax.ppermute(down, "lev", [(i + 1, i) for i in range(levels - 1)])
     atm_next, ocean_next, atm_base, ocean_base = pl.pallas_call(
@@ -234,7 +234,7 @@
             shape((16, 256), f32),
             shape((64, 128), f32),
         ),
-        in_specs=[smem] * 2 + [vmem] * 5,
+        in_specs=[vmem] * 7,
         out_specs=(hbm, hbm, vmem, vmem),
         scratch_shapes=[
             pltpu.VMEM(atm_state.shape, f32),
@@ -255,7 +255,7 @@
         ],
         input_output_aliases={0: 0, 1: 1},
         compiler_params=params,
-    )(atm_next, ocean_next, atm_base, ocean_base, own, previous, following)
+    )(atm_next, ocean_next, atm_base, ocean_base, own, second, first)
     ocean_next = ocean_next.reshape(2, 32, 2, 128).transpose(0, 2, 1, 3).reshape(ocean_state.shape)
     return (atm_next, ocean_next)
 

time: 38 us -> 37.6 us (0.989)
  Pallas kernels: 3.99 us -> 3.58 us
    pallas_call x1, Pallas kernels: 1.54 us -> 1.06 us  [shards(): pl.pallas_call(column_kernel, out_shape=(shape(atm_state.shape, f32), sha...]
  transfers between devices with their start and end apart: 5 -> 5, of which waited for: 0 -> 0; matrix products, arithmetic and copies ran while one was open for 0% -> 0% of each run, Pallas kernels for 4% -> 3%
where the time goes in v3:
time: 37.6 us; the launch traced here: 37.3 us
  starting transfers between devices  32.9 us (88%)
  Pallas kernels  3.58 us (10%)
  between operations  0.8 us (2%)
    all_to_all x1, starting transfers between devices, shards(): lax.all_to_all(send, ('horiz', 'lev'), 0, 0, axis_index_groups=pairs, til...  16.2 us
    ppermute x2, starting transfers between devices, swap(): return lax.ppermute(own, ('horiz', 'lev'), pairs)  11.1 us
    ppermute x1, starting transfers between devices, shards(): above = lax.ppermute(down, 'lev', [(i + 1, i) for i in range(levels - 1)])  3.5 us
    pallas_call x1, Pallas kernels, shards(): pl.pallas_call(prep_kernel, out_shape=(shape((128, 128), bf16), shape((12...  2.48 us
    ppermute x1, starting transfers between devices, shards(): below = lax.ppermute(up, 'lev', [(i, i + 1) for i in range(levels - 1)])  2.04 us
    pallas_call x1, Pallas kernels, shards(): pl.pallas_call(column_kernel, out_shape=(shape(atm_state.shape, f32), sha...  1.06 us
  transfers between devices with their start and end apart: 5, of which 0 were waited for; matrix products, arithmetic and copies ran while one was open for 0% of the time, Pallas kernels for 3%

profile of v3, /device:TPU:38, one launch (start us, length us, event | category | flops | bytes accessed | tf_op | source)
XLA Modules:
  0.0 37.3 jit_solution(10534456731854006798)
XLA Ops:
  0.6 0.0 copy-start
  0.6 2.5 %shard_map.140 = (bf16[128,128]{1,0:T(8,128)(2,1)}, f32[12,16,128]{2,1,0:T(8,128)}, f32[12,16,128]{2,1,0:T(8,128)}) custom-call(s32[10]{0:T(128)} %ocean_src_hbm.1, s32[10]{0:T(128)} %ocean_dst_hbm.1, s32[10]{0:T(128)} %atmos_src_hbm.1, s32[10]{0:T(128)} %atmos_dst_hbm.1, f32[4,2,16,256]{3,2,1,0:T(8,128)} %atm.1, f32[128,128]{1,0:T(8,128)} %bitcast.14, ...), custom_call_target="tpu_custom_call" | custom-call | tf_op jit(solution)/shard_map/pallas_call | solution.py:187
  3.1 0.0 copy-start.1
  3.1 0.0 copy-start.2
  3.2 16.2 %all-to-all-start = ((bf16[16,8,128]{2,1,0:T(8,128)(2,1)}), bf16[16,8,128]{2,1,0:T(8,128)(2,1)S(1)}, u32[]{:S(2)}, u32[]{:S(2)}) async-start(bf16[16,8,128]{2,1,0:T(8,128)(2,1)} %bitcast.21), calls=%async_computation | async-start | bytes 65536 | tf_op jit(solution)/shard_map/all_to_all | solution.py:213
  19.4 2.0 %collective-permute-start = (f32[12,16,128]{2,1,0:T(8,128)}, f32[12,16,128]{2,1,0:T(8,128)S(1)}, u32[]{:S(2)}, u32[]{:S(2)}) collective-permute-start(f32[12,16,128]{2,1,0:T(8,128)} %get-tuple-element.11), channel_id=1, source_target_pairs={{0,1},{1,2},{2,3},{3,4},{4,5},{5,6},{6,7},{8,9},{9,10},{10,11},{11... | collective-permute-start | bytes 294920 | tf_op jit(solution)/shard_map/ppermute | solution.py:227
  21.4 3.5 %collective-permute-start.1 = (f32[12,16,128]{2,1,0:T(8,128)}, f32[12,16,128]{2,1,0:T(8,128)S(1)}, u32[]{:S(2)}, u32[]{:S(2)}) collective-permute-start(f32[12,16,128]{2,1,0:T(8,128)} %get-tuple-element.12), channel_id=1, source_target_pairs={{1,0},{2,1},{3,2},{4,3},{5,4},{6,5},{7,6},{9,8},{10,9},{11,10},{12... | collective-permute-start | bytes 294920 | tf_op jit(solution)/shard_map/ppermute | solution.py:228
  24.9 0.0 all-to-all-done
  24.9 0.0 copy-start.4
  24.9 0.0 copy-start.3
  25.0 10.5 %collective-permute-start.3 = (bf16[128,128]{1,0:T(8,128)(2,1)S(1)}, bf16[128,128]{1,0:T(8,128)(2,1)S(1)}, u32[]{:S(2)}, u32[]{:S(2)}) collective-permute-start(bf16[128,128]{1,0:T(8,128)(2,1)S(1)} %bitcast.16), channel_id=1, source_target_pairs={{17,32},{46,16},{25,40},{42,24},{49,64},{78,48},{57,72},{74,56},{8... | collective-permute-start | bytes 98312 | tf_op jit(solution)/shard_map/ppermute | solution.py:223
  35.4 0.7 %collective-permute-start.2 = (bf16[128,128]{1,0:T(8,128)(2,1)S(1)}, bf16[128,128]{1,0:T(8,128)(2,1)S(1)}, u32[]{:S(2)}, u32[]{:S(2)}) collective-permute-start(bf16[128,128]{1,0:T(8,128)(2,1)S(1)} %bitcast.17), channel_id=1, source_target_pairs={{1,16},{30,0},{9,24},{26,8},{33,48},{62,32},{41,56},{58,40},{65,80... | collective-permute-start | bytes 98312 | tf_op jit(solution)/shard_map/ppermute | solution.py:223
  36.1 0.0 collective-permute-done.below
  36.1 0.0 collective-permute-done.1.above
  36.1 0.0 copy-done
  36.1 0.0 copy-done.1
  36.1 0.0 copy-done.2
  36.1 0.0 copy-done.4
  36.2 0.0 copy-done.3
  36.2 1.1 %shard_map.141 = (f32[4,2,16,256]{3,2,1,0:T(8,128)}, f32[128,128]{1,0:T(8,128)}, f32[16,256]{1,0:T(8,128)S(1)}, f32[64,128]{1,0:T(8,128)S(1)}) custom-call(f32[2,4]{1,0:T(2,128)S(1)} %bitcast.19, f32[2,2]{1,0:T(2,128)S(1)} %copy-done.4, f32[4,2,16,256]{3,2,1,0:T(8,128)S(1)} %copy-done, f32[128,128]{1,0:T(8,128)S(1)} %bitcast.15, f32[16,16]{1,0:T(8,128)S(1)} %copy-done.2, ...), custom_call_target="tpu_custom_call" | custom-call | tf_op jit(solution)/shard_map/pallas_call | solution.py:229
  37.2 0.0 collective-permute-done.3.first
  37.2 0.0 collective-permute-done.2.second
  (1 shorter events, 0.0 us)
Async XLA Ops:
  0.6 35.5 %copy-start = (f32[4,2,16,256]{3,2,1,0:T(8,128)S(1)}, f32[4,2,16,256]{3,2,1,0:T(8,128)}, u32[]{:S(2)}) copy-start(f32[4,2,16,256]{3,2,1,0:T(8,128)} %atm.1) | copy-start | bytes 393220
  3.1 33.0 %copy-start.1 = (f32[2,2,4096]{2,1,0:T(2,128)S(1)}, f32[2,2,4096]{2,1,0:T(2,128)}, u32[]{:S(2)}) copy-start(f32[2,2,4096]{2,1,0:T(2,128)} %param.16) | copy-start | bytes 196612
  3.1 33.0 %copy-start.2 = (f32[16,16]{1,0:T(8,128)S(1)}, f32[16,16]{1,0:T(8,128)}, u32[]{:S(2)}) copy-start(f32[16,16]{1,0:T(8,128)} %operator.1) | copy-start | bytes 3076
  3.2 21.8 %all-to-all-start = ((bf16[16,8,128]{2,1,0:T(8,128)(2,1)}), bf16[16,8,128]{2,1,0:T(8,128)(2,1)S(1)}, u32[]{:S(2)}, u32[]{:S(2)}) async-start(bf16[16,8,128]{2,1,0:T(8,128)(2,1)} %bitcast.21), calls=%async_computation | async-start | bytes 65536 | tf_op jit(solution)/shard_map/all_to_all | solution.py:213
  19.4 16.7 %collective-permute-start = (f32[12,16,128]{2,1,0:T(8,128)}, f32[12,16,128]{2,1,0:T(8,128)S(1)}, u32[]{:S(2)}, u32[]{:S(2)}) collective-permute-start(f32[12,16,128]{2,1,0:T(8,128)} %get-tuple-element.11), channel_id=1, source_target_pairs={{0,1},{1,2},{2,3},{3,4},{4,5},{5,6},{6,7},{8,9},{9,10},{10,11},{11... | collective-permute-start | bytes 294920 | tf_op jit(solution)/shard_map/ppermute | solution.py:227
  21.4 14.7 %collective-permute-start.1 = (f32[12,16,128]{2,1,0:T(8,128)}, f32[12,16,128]{2,1,0:T(8,128)S(1)}, u32[]{:S(2)}, u32[]{:S(2)}) collective-permute-start(f32[12,16,128]{2,1,0:T(8,128)} %get-tuple-element.12), channel_id=1, source_target_pairs={{1,0},{2,1},{3,2},{4,3},{5,4},{6,5},{7,6},{9,8},{10,9},{11,10},{12... | collective-permute-start | bytes 294920 | tf_op jit(solution)/shard_map/ppermute | solution.py:228
  24.9 11.2 %copy-start.4 = (f32[2,2]{1,0:T(2,128)S(1)}, f32[2,2]{1,0:T(2,128)}, u32[]{:S(2)}) copy-start(f32[2,2]{1,0:T(2,128)} %ocean_mixing.1) | copy-start | bytes 52
  24.9 11.2 %copy-start.3 = (f32[4,2]{0,1:T(2,128)S(1)}, f32[4,2]{0,1:T(2,128)}, u32[]{:S(2)}) copy-start(f32[4,2]{0,1:T(2,128)} %param.14) | copy-start | bytes 100
  25.0 12.3 %collective-permute-start.3 = (bf16[128,128]{1,0:T(8,128)(2,1)S(1)}, bf16[128,128]{1,0:T(8,128)(2,1)S(1)}, u32[]{:S(2)}, u32[]{:S(2)}) collective-permute-start(bf16[128,128]{1,0:T(8,128)(2,1)S(1)} %bitcast.16), channel_id=1, source_target_pairs={{17,32},{46,16},{25,40},{42,24},{49,64},{78,48},{57,72},{74,56},{8... | collective-permute-start | bytes 98312 | tf_op jit(solution)/shard_map/ppermute | solution.py:223
  35.4 1.8 %collective-permute-start.2 = (bf16[128,128]{1,0:T(8,128)(2,1)S(1)}, bf16[128,128]{1,0:T(8,128)(2,1)S(1)}, u32[]{:S(2)}, u32[]{:S(2)}) collective-permute-start(bf16[128,128]{1,0:T(8,128)(2,1)S(1)} %bitcast.17), channel_id=1, source_target_pairs={{1,16},{30,0},{9,24},{26,8},{33,48},{62,32},{41,56},{58,40},{65,80... | collective-permute-start | bytes 98312 | tf_op jit(solution)/shard_map/ppermute | solution.py:223

commit v4 on v3

--- a/solution.py
+++ b/solution.py
@@ -12,6 +12,10 @@
 NEXT = ((0, 1), (1, 1))
 PREVIOUS = ((1, 6), (1, 2))
 EMPTY = 64
+
+
+def seat(level):
+    return 7 - level
 
 
 def prep_kernel(
@@ -41,7 +45,7 @@
         copy.wait()
     lane = lax.broadcasted_iota(jnp.int32, (4, 128), 1)
     line = lax.broadcasted_iota(jnp.int32, (4, 128), 0)
-    inside = lane % 64 - 8 * level
+    inside = lane % 64 - 8 * seat(level)
     codes = jnp.where((inside >= 0) & (inside < 8), EMPTY, 0)
     for reach in range(REACH):
         delta = reach - NEAR
@@ -57,7 +61,7 @@
             to = atmos_dst[reach * CAP + place]
             code = jnp.where(to < 32, 32 + (to % 2) * 16 + to // 2, EMPTY)
             codes = jnp.where(here & (inside == CAP + place), code, codes)
-    rows_out[pl.ds(64 * odd + 4, 4), :] = codes.astype(jnp.float32)
+    rows_out[pl.ds(64 * odd + 8 * seat(0) + 4, 4), :] = codes.astype(jnp.float32)
     picks[0:16] = flux[:, 0:128].astype(jnp.float32)
     picks[16:32] = flux[:, 128:256].astype(jnp.float32)
     picks[32:64] = sea[...].astype(jnp.float32)
@@ -70,7 +74,7 @@
     def chunk(reach):
         def member(target):
             column, lev = PREVIOUS[target + 2] if target < 0 else NEXT[target - 2] if target > 1 else (target, 0)
-            return column * 8 + lev
+            return column * 8 + seat(lev)
 
         return 8 * jnp.where(odd == 0, member(reach - NEAR), member(reach - NEAR + 1))
 
@@ -209,7 +213,7 @@
         ocean_tile_src, ocean_tile_dst, atmos_tile_src, atmos_tile_dst,
         atm_state, ocean_rows, atm_flux, sea_temp.reshape(32, 128), ocean_tiles, atmos_tiles,
     )
-    pairs = [[h * levels + l for h in (g, g + 1) for l in range(levels)] for g in range(0, columns, 2)]
+    pairs = [[h * levels + 7 - l for h in (g, g + 1) for l in range(levels)] for g in range(0, columns, 2)]
     own = lax.all_to_all(send, ("horiz", "lev"), 0, 0, axis_index_groups=pairs, tiled=True)
 
     def swap(wave):

time: 37.6 us -> 37 us (0.984)
  the two profiles are of different devices: /device:TPU:38 before, /device:TPU:32 now
where the time goes in v4:
time: 37 us; the launch traced here: 36.6 us
  starting transfers between devices  22.5 us (61%)
  waiting for transfers between devices  9.01 us (24%)
  Pallas kernels  4.35 us (12%)
  between operations  0.78 us (2%)
    all_to_all x1, starting transfers between devices, shards(): lax.all_to_all(send, ('horiz', 'lev'), 0, 0, axis_index_groups=pairs, til...  16.6 us
    ppermute x2, waiting for transfers between devices, swap(): return lax.ppermute(own, ('horiz', 'lev'), pairs)  9 us
    ppermute x2, starting transfers between devices, swap(): return lax.ppermute(own, ('horiz', 'lev'), pairs)  2.58 us
    pallas_call x1, Pallas kernels, shards(): pl.pallas_call(prep_kernel, out_shape=(shape((128, 128), bf16), shape((12...  2.48 us
    ppermute x1, starting transfers between devices, shards(): below = lax.ppermute(up, 'lev', [(i, i + 1) for i in range(levels - 1)])  1.98 us
    ppermute x1, starting transfers between devices, shards(): above = lax.ppermute(down, 'lev', [(i + 1, i) for i in range(levels - 1)])  1.29 us
    pallas_call x1, Pallas kernels, shards(): pl.pallas_call(column_kernel, out_shape=(shape(atm_state.shape, f32), sha...  1.06 us
    pallas_call x1, Pallas kernels, shards(): pl.pallas_call(surface_kernel, out_shape=(shape(atm_state.shape, f32), sh...  0.8 us
  transfers between devices with their start and end apart: 5, of which 1 were waited for; matrix products, arithmetic and copies ran while one was open for 0% of the time, Pallas kernels for 3%

profile of v4, /device:TPU:32, one launch (start us, length us, event | category | flops | bytes accessed | tf_op | source)
XLA Modules:
  0.0 36.6 jit_solution(5742134740785112728)
XLA Ops:
  0.6 0.0 copy-start
  0.6 2.5 %shard_map.140 = (bf16[128,128]{1,0:T(8,128)(2,1)}, f32[12,16,128]{2,1,0:T(8,128)}, f32[12,16,128]{2,1,0:T(8,128)}) custom-call(s32[10]{0:T(128)} %ocean_src_hbm.1, s32[10]{0:T(128)} %ocean_dst_hbm.1, s32[10]{0:T(128)} %atmos_src_hbm.1, s32[10]{0:T(128)} %atmos_dst_hbm.1, f32[4,2,16,256]{3,2,1,0:T(8,128)} %atm.1, f32[128,128]{1,0:T(8,128)} %bitcast.14, ...), custom_call_target="tpu_custom_call" | custom-call | tf_op jit(solution)/shard_map/pallas_call | solution.py:191
  3.1 0.0 copy-start.1
  3.1 0.0 copy-start.2
  3.2 16.6 %all-to-all-start = ((bf16[16,8,128]{2,1,0:T(8,128)(2,1)}), bf16[16,8,128]{2,1,0:T(8,128)(2,1)S(1)}, u32[]{:S(2)}, u32[]{:S(2)}) async-start(bf16[16,8,128]{2,1,0:T(8,128)(2,1)} %bitcast.21), calls=%async_computation | async-start | bytes 65536 | tf_op jit(solution)/shard_map/all_to_all | solution.py:217
  19.8 2.0 %collective-permute-start = (f32[12,16,128]{2,1,0:T(8,128)}, f32[12,16,128]{2,1,0:T(8,128)S(1)}, u32[]{:S(2)}, u32[]{:S(2)}) collective-permute-start(f32[12,16,128]{2,1,0:T(8,128)} %get-tuple-element.11), channel_id=1, source_target_pairs={{0,1},{1,2},{2,3},{3,4},{4,5},{5,6},{6,7},{8,9},{9,10},{10,11},{11... | collective-permute-start | bytes 294920 | tf_op jit(solution)/shard_map/ppermute | solution.py:231
  21.8 1.3 %collective-permute-start.1 = (f32[12,16,128]{2,1,0:T(8,128)}, f32[12,16,128]{2,1,0:T(8,128)S(1)}, u32[]{:S(2)}, u32[]{:S(2)}) collective-permute-start(f32[12,16,128]{2,1,0:T(8,128)} %get-tuple-element.12), channel_id=1, source_target_pairs={{1,0},{2,1},{3,2},{4,3},{5,4},{6,5},{7,6},{9,8},{10,9},{11,10},{12... | collective-permute-start | bytes 294920 | tf_op jit(solution)/shard_map/ppermute | solution.py:232
  23.1 0.0 all-to-all-done
  23.1 0.0 copy-start.4
  23.1 0.0 copy-start.3
  23.1 1.3 %collective-permute-start.3 = (bf16[128,128]{1,0:T(8,128)(2,1)S(1)}, bf16[128,128]{1,0:T(8,128)(2,1)S(1)}, u32[]{:S(2)}, u32[]{:S(2)}) collective-permute-start(bf16[128,128]{1,0:T(8,128)(2,1)S(1)} %bitcast.16), channel_id=1, source_target_pairs={{17,32},{46,16},{25,40},{42,24},{49,64},{78,48},{57,72},{74,56},{8... | collective-permute-start | bytes 98312 | tf_op jit(solution)/shard_map/ppermute | solution.py:227
  24.4 1.3 %collective-permute-start.2 = (bf16[128,128]{1,0:T(8,128)(2,1)S(1)}, bf16[128,128]{1,0:T(8,128)(2,1)S(1)}, u32[]{:S(2)}, u32[]{:S(2)}) collective-permute-start(bf16[128,128]{1,0:T(8,128)(2,1)S(1)} %bitcast.17), channel_id=1, source_target_pairs={{1,16},{30,0},{9,24},{26,8},{33,48},{62,32},{41,56},{58,40},{65,80... | collective-permute-start | bytes 98312 | tf_op jit(solution)/shard_map/ppermute | solution.py:227
  25.7 0.0 collective-permute-done.below
  25.7 0.0 collective-permute-done.1.above
  25.7 0.0 copy-done
  25.7 0.0 copy-done.1
  25.7 0.0 copy-done.2
  25.8 0.0 copy-done.4
  25.8 0.0 copy-done.3
  25.8 1.1 %shard_map.141 = (f32[4,2,16,256]{3,2,1,0:T(8,128)}, f32[128,128]{1,0:T(8,128)}, f32[16,256]{1,0:T(8,128)S(1)}, f32[64,128]{1,0:T(8,128)S(1)}) custom-call(f32[2,4]{1,0:T(2,128)S(1)} %bitcast.19, f32[2,2]{1,0:T(2,128)S(1)} %copy-done.4, f32[4,2,16,256]{3,2,1,0:T(8,128)S(1)} %copy-done, f32[128,128]{1,0:T(8,128)S(1)} %bitcast.15, f32[16,16]{1,0:T(8,128)S(1)} %copy-done.2, ...), custom_call_target="tpu_custom_call" | custom-call | tf_op jit(solution)/shard_map/pallas_call | solution.py:233
  26.8 9.0 %collective-permute-done.3.first = bf16[128,128]{1,0:T(8,128)(2,1)S(1)} collective-permute-done((bf16[128,128]{1,0:T(8,128)(2,1)S(1)}, bf16[128,128]{1,0:T(8,128)(2,1)S(1)}, u32[]{:S(2)}, u32[]{:S(2)}) %collective-permute-start.3) | collective-permute-done | bytes 32800 | tf_op jit(solution)/shard_map/ppermute | solution.py:227
  35.8 0.0 collective-permute-done.2.second
  35.8 0.8 %shard_map.142 = (f32[4,2,16,256]{3,2,1,0:T(8,128)}, f32[128,128]{1,0:T(8,128)}) custom-call(f32[4,2,16,256]{3,2,1,0:T(8,128)} %get-tuple-element.13.atm_in, f32[128,128]{1,0:T(8,128)} %get-tuple-element.14.ocean_in, f32[16,256]{1,0:T(8,128)S(1)} %get-tuple-element.15.atm_base, ...), custom_call_target="tpu_custom_call", output_to_operand_aliasing={{0}: (0, {}), {1}: (1, {})} | custom-call | tf_op jit(solution)/shard_map/pallas_call | solution.py:250
Async XLA Ops:
  0.6 25.1 %copy-start = (f32[4,2,16,256]{3,2,1,0:T(8,128)S(1)}, f32[4,2,16,256]{3,2,1,0:T(8,128)}, u32[]{:S(2)}) copy-start(f32[4,2,16,256]{3,2,1,0:T(8,128)} %atm.1) | copy-start | bytes 393220
  3.1 22.6 %copy-start.1 = (f32[2,2,4096]{2,1,0:T(2,128)S(1)}, f32[2,2,4096]{2,1,0:T(2,128)}, u32[]{:S(2)}) copy-start(f32[2,2,4096]{2,1,0:T(2,128)} %param.16) | copy-start | bytes 196612
  3.1 22.6 %copy-start.2 = (f32[16,16]{1,0:T(8,128)S(1)}, f32[16,16]{1,0:T(8,128)}, u32[]{:S(2)}) copy-start(f32[16,16]{1,0:T(8,128)} %operator.1) | copy-start | bytes 3076
  3.2 19.9 %all-to-all-start = ((bf16[16,8,128]{2,1,0:T(8,128)(2,1)}), bf16[16,8,128]{2,1,0:T(8,128)(2,1)S(1)}, u32[]{:S(2)}, u32[]{:S(2)}) async-start(bf16[16,8,128]{2,1,0:T(8,128)(2,1)} %bitcast.21), calls=%async_computation | async-start | bytes 65536 | tf_op jit(solution)/shard_map/all_to_all | solution.py:217
  19.8 5.9 %collective-permute-start = (f32[12,16,128]{2,1,0:T(8,128)}, f32[12,16,128]{2,1,0:T(8,128)S(1)}, u32[]{:S(2)}, u32[]{:S(2)}) collective-permute-start(f32[12,16,128]{2,1,0:T(8,128)} %get-tuple-element.11), channel_id=1, source_target_pairs={{0,1},{1,2},{2,3},{3,4},{4,5},{5,6},{6,7},{8,9},{9,10},{10,11},{11... | collective-permute-start | bytes 294920 | tf_op jit(solution)/shard_map/ppermute | solution.py:231
  21.8 3.9 %collective-permute-start.1 = (f32[12,16,128]{2,1,0:T(8,128)}, f32[12,16,128]{2,1,0:T(8,128)S(1)}, u32[]{:S(2)}, u32[]{:S(2)}) collective-permute-start(f32[12,16,128]{2,1,0:T(8,128)} %get-tuple-element.12), channel_id=1, source_target_pairs={{1,0},{2,1},{3,2},{4,3},{5,4},{6,5},{7,6},{9,8},{10,9},{11,10},{12... | collective-permute-start | bytes 294920 | tf_op jit(solution)/shard_map/ppermute | solution.py:232
  23.1 2.7 %copy-start.4 = (f32[2,2]{1,0:T(2,128)S(1)}, f32[2,2]{1,0:T(2,128)}, u32[]{:S(2)}) copy-start(f32[2,2]{1,0:T(2,128)} %ocean_mixing.1) | copy-start | bytes 52
  23.1 2.7 %copy-start.3 = (f32[4,2]{0,1:T(2,128)S(1)}, f32[4,2]{0,1:T(2,128)}, u32[]{:S(2)}) copy-start(f32[4,2]{0,1:T(2,128)} %param.14) | copy-start | bytes 100
  23.1 12.7 %collective-permute-start.3 = (bf16[128,128]{1,0:T(8,128)(2,1)S(1)}, bf16[128,128]{1,0:T(8,128)(2,1)S(1)}, u32[]{:S(2)}, u32[]{:S(2)}) collective-permute-start(bf16[128,128]{1,0:T(8,128)(2,1)S(1)} %bitcast.16), channel_id=1, source_target_pairs={{17,32},{46,16},{25,40},{42,24},{49,64},{78,48},{57,72},{74,56},{8... | collective-permute-start | bytes 98312 | tf_op jit(solution)/shard_map/ppermute | solution.py:227
  24.4 11.4 %collective-permute-start.2 = (bf16[128,128]{1,0:T(8,128)(2,1)S(1)}, bf16[128,128]{1,0:T(8,128)(2,1)S(1)}, u32[]{:S(2)}, u32[]{:S(2)}) collective-permute-start(bf16[128,128]{1,0:T(8,128)(2,1)S(1)} %bitcast.17), channel_id=1, source_target_pairs={{1,16},{30,0},{9,24},{26,8},{33,48},{62,32},{41,56},{58,40},{65,80... | collective-permute-start | bytes 98312 | tf_op jit(solution)/shard_map/ppermute | solution.py:227

commit v5 on v4

--- a/solution.py
+++ b/solution.py
@@ -9,7 +9,7 @@
 NEAR = 2
 CAP = 2
 REACH = 2 * NEAR + 1
-NEXT = ((0, 1), (1, 1))
+NEXT = ((0, 1), (1, 7))
 PREVIOUS = ((1, 6), (1, 2))
 EMPTY = 64
 

time: 37 us -> 36.8 us (level)
  no operation moved by 1% of the time
where the time goes in v5:
time: 36.8 us; the launch traced here: 36.4 us
  starting transfers between devices  22.5 us (61%)
  waiting for transfers between devices  8.79 us (24%)
  Pallas kernels  4.36 us (12%)
  between operations  0.78 us (2%)
    all_to_all x1, starting transfers between devices, shards(): lax.all_to_all(send, ('horiz', 'lev'), 0, 0, axis_index_groups=pairs, til...  16.6 us
    ppermute x2, waiting for transfers between devices, swap(): return lax.ppermute(own, ('horiz', 'lev'), pairs)  8.79 us
    ppermute x2, starting transfers between devices, swap(): return lax.ppermute(own, ('horiz', 'lev'), pairs)  2.58 us
    pallas_call x1, Pallas kernels, shards(): pl.pallas_call(prep_kernel, out_shape=(shape((128, 128), bf16), shape((12...  2.48 us
    ppermute x1, starting transfers between devices, shards(): below = lax.ppermute(up, 'lev', [(i, i + 1) for i in range(levels - 1)])  1.98 us
    ppermute x1, starting transfers between devices, shards(): above = lax.ppermute(down, 'lev', [(i + 1, i) for i in range(levels - 1)])  1.29 us
    pallas_call x1, Pallas kernels, shards(): pl.pallas_call(column_kernel, out_shape=(shape(atm_state.shape, f32), sha...  1.08 us
    pallas_call x1, Pallas kernels, shards(): pl.pallas_call(surface_kernel, out_shape=(shape(atm_state.shape, f32), sh...  0.8 us
  transfers between devices with their start and end apart: 5, of which 1 were waited for; matrix products, arithmetic and copies ran while one was open for 0% of the time, Pallas kernels for 3%

profile of v5, /device:TPU:32, one launch (start us, length us, event | category | flops | bytes accessed | tf_op | source)
XLA Modules:
  0.0 36.4 jit_solution(10911449474814296433)
XLA Ops:
  0.6 0.0 copy-start
  0.6 2.5 %shard_map.140 = (bf16[128,128]{1,0:T(8,128)(2,1)}, f32[12,16,128]{2,1,0:T(8,128)}, f32[12,16,128]{2,1,0:T(8,128)}) custom-call(s32[10]{0:T(128)} %ocean_src_hbm.1, s32[10]{0:T(128)} %ocean_dst_hbm.1, s32[10]{0:T(128)} %atmos_src_hbm.1, s32[10]{0:T(128)} %atmos_dst_hbm.1, f32[4,2,16,256]{3,2,1,0:T(8,128)} %atm.1, f32[128,128]{1,0:T(8,128)} %bitcast.14, ...), custom_call_target="tpu_custom_call" | custom-call | tf_op jit(solution)/shard_map/pallas_call | solution.py:191
  3.1 0.0 copy-start.1
  3.1 0.0 copy-start.2
  3.2 16.6 %all-to-all-start = ((bf16[16,8,128]{2,1,0:T(8,128)(2,1)}), bf16[16,8,128]{2,1,0:T(8,128)(2,1)S(1)}, u32[]{:S(2)}, u32[]{:S(2)}) async-start(bf16[16,8,128]{2,1,0:T(8,128)(2,1)} %bitcast.21), calls=%async_computation | async-start | bytes 65536 | tf_op jit(solution)/shard_map/all_to_all | solution.py:217
  19.8 2.0 %collective-permute-start = (f32[12,16,128]{2,1,0:T(8,128)}, f32[12,16,128]{2,1,0:T(8,128)S(1)}, u32[]{:S(2)}, u32[]{:S(2)}) collective-permute-start(f32[12,16,128]{2,1,0:T(8,128)} %get-tuple-element.11), channel_id=1, source_target_pairs={{0,1},{1,2},{2,3},{3,4},{4,5},{5,6},{6,7},{8,9},{9,10},{10,11},{11... | collective-permute-start | bytes 294920 | tf_op jit(solution)/shard_map/ppermute | solution.py:231
  21.8 1.3 %collective-permute-start.1 = (f32[12,16,128]{2,1,0:T(8,128)}, f32[12,16,128]{2,1,0:T(8,128)S(1)}, u32[]{:S(2)}, u32[]{:S(2)}) collective-permute-start(f32[12,16,128]{2,1,0:T(8,128)} %get-tuple-element.12), channel_id=1, source_target_pairs={{1,0},{2,1},{3,2},{4,3},{5,4},{6,5},{7,6},{9,8},{10,9},{11,10},{12... | collective-permute-start | bytes 294920 | tf_op jit(solution)/shard_map/ppermute | solution.py:232
  23.1 0.0 all-to-all-done
  23.1 0.0 copy-start.4
  23.1 0.0 copy-start.3
  23.1 1.3 %collective-permute-start.3 = (bf16[128,128]{1,0:T(8,128)(2,1)S(1)}, bf16[128,128]{1,0:T(8,128)(2,1)S(1)}, u32[]{:S(2)}, u32[]{:S(2)}) collective-permute-start(bf16[128,128]{1,0:T(8,128)(2,1)S(1)} %bitcast.16), channel_id=1, source_target_pairs={{17,32},{46,16},{31,40},{42,24},{49,64},{78,48},{63,72},{74,56},{8... | collective-permute-start | bytes 98312 | tf_op jit(solution)/shard_map/ppermute | solution.py:227
  24.4 1.3 %collective-permute-start.2 = (bf16[128,128]{1,0:T(8,128)(2,1)S(1)}, bf16[128,128]{1,0:T(8,128)(2,1)S(1)}, u32[]{:S(2)}, u32[]{:S(2)}) collective-permute-start(bf16[128,128]{1,0:T(8,128)(2,1)S(1)} %bitcast.17), channel_id=1, source_target_pairs={{1,16},{30,0},{15,24},{26,8},{33,48},{62,32},{47,56},{58,40},{65,8... | collective-permute-start | bytes 98312 | tf_op jit(solution)/shard_map/ppermute | solution.py:227
  25.7 0.0 collective-permute-done.below
  25.7 0.0 collective-permute-done.1.above
  25.7 0.0 copy-done
  25.7 0.0 copy-done.1
  25.7 0.0 copy-done.2
  25.8 0.0 copy-done.4
  25.8 0.0 copy-done.3
  25.8 1.1 %shard_map.141 = (f32[4,2,16,256]{3,2,1,0:T(8,128)}, f32[128,128]{1,0:T(8,128)}, f32[16,256]{1,0:T(8,128)S(1)}, f32[64,128]{1,0:T(8,128)S(1)}) custom-call(f32[2,4]{1,0:T(2,128)S(1)} %bitcast.19, f32[2,2]{1,0:T(2,128)S(1)} %copy-done.4, f32[4,2,16,256]{3,2,1,0:T(8,128)S(1)} %copy-done, f32[128,128]{1,0:T(8,128)S(1)} %bitcast.15, f32[16,16]{1,0:T(8,128)S(1)} %copy-done.2, ...), custom_call_target="tpu_custom_call" | custom-call | tf_op jit(solution)/shard_map/pallas_call | solution.py:233
  26.9 8.8 %collective-permute-done.3.first = bf16[128,128]{1,0:T(8,128)(2,1)S(1)} collective-permute-done((bf16[128,128]{1,0:T(8,128)(2,1)S(1)}, bf16[128,128]{1,0:T(8,128)(2,1)S(1)}, u32[]{:S(2)}, u32[]{:S(2)}) %collective-permute-start.3) | collective-permute-done | bytes 32800 | tf_op jit(solution)/shard_map/ppermute | solution.py:227
  35.6 0.0 collective-permute-done.2.second
  35.6 0.8 %shard_map.142 = (f32[4,2,16,256]{3,2,1,0:T(8,128)}, f32[128,128]{1,0:T(8,128)}) custom-call(f32[4,2,16,256]{3,2,1,0:T(8,128)} %get-tuple-element.13.atm_in, f32[128,128]{1,0:T(8,128)} %get-tuple-element.14.ocean_in, f32[16,256]{1,0:T(8,128)S(1)} %get-tuple-element.15.atm_base, ...), custom_call_target="tpu_custom_call", output_to_operand_aliasing={{0}: (0, {}), {1}: (1, {})} | custom-call | tf_op jit(solution)/shard_map/pallas_call | solution.py:250
Async XLA Ops:
  0.6 25.1 %copy-start = (f32[4,2,16,256]{3,2,1,0:T(8,128)S(1)}, f32[4,2,16,256]{3,2,1,0:T(8,128)}, u32[]{:S(2)}) copy-start(f32[4,2,16,256]{3,2,1,0:T(8,128)} %atm.1) | copy-start | bytes 393220
  3.1 22.6 %copy-start.1 = (f32[2,2,4096]{2,1,0:T(2,128)S(1)}, f32[2,2,4096]{2,1,0:T(2,128)}, u32[]{:S(2)}) copy-start(f32[2,2,4096]{2,1,0:T(2,128)} %param.16) | copy-start | bytes 196612
  3.1 22.6 %copy-start.2 = (f32[16,16]{1,0:T(8,128)S(1)}, f32[16,16]{1,0:T(8,128)}, u32[]{:S(2)}) copy-start(f32[16,16]{1,0:T(8,128)} %operator.1) | copy-start | bytes 3076
  3.2 19.9 %all-to-all-start = ((bf16[16,8,128]{2,1,0:T(8,128)(2,1)}), bf16[16,8,128]{2,1,0:T(8,128)(2,1)S(1)}, u32[]{:S(2)}, u32[]{:S(2)}) async-start(bf16[16,8,128]{2,1,0:T(8,128)(2,1)} %bitcast.21), calls=%async_computation | async-start | bytes 65536 | tf_op jit(solution)/shard_map/all_to_all | solution.py:217
  19.8 5.9 %collective-permute-start = (f32[12,16,128]{2,1,0:T(8,128)}, f32[12,16,128]{2,1,0:T(8,128)S(1)}, u32[]{:S(2)}, u32[]{:S(2)}) collective-permute-start(f32[12,16,128]{2,1,0:T(8,128)} %get-tuple-element.11), channel_id=1, source_target_pairs={{0,1},{1,2},{2,3},{3,4},{4,5},{5,6},{6,7},{8,9},{9,10},{10,11},{11... | collective-permute-start | bytes 294920 | tf_op jit(solution)/shard_map/ppermute | solution.py:231
  21.8 3.9 %collective-permute-start.1 = (f32[12,16,128]{2,1,0:T(8,128)}, f32[12,16,128]{2,1,0:T(8,128)S(1)}, u32[]{:S(2)}, u32[]{:S(2)}) collective-permute-start(f32[12,16,128]{2,1,0:T(8,128)} %get-tuple-element.12), channel_id=1, source_target_pairs={{1,0},{2,1},{3,2},{4,3},{5,4},{6,5},{7,6},{9,8},{10,9},{11,10},{12... | collective-permute-start | bytes 294920 | tf_op jit(solution)/shard_map/ppermute | solution.py:232
  23.1 2.7 %copy-start.4 = (f32[2,2]{1,0:T(2,128)S(1)}, f32[2,2]{1,0:T(2,128)}, u32[]{:S(2)}) copy-start(f32[2,2]{1,0:T(2,128)} %ocean_mixing.1) | copy-start | bytes 52
  23.1 2.7 %copy-start.3 = (f32[4,2]{0,1:T(2,128)S(1)}, f32[4,2]{0,1:T(2,128)}, u32[]{:S(2)}) copy-start(f32[4,2]{0,1:T(2,128)} %param.14) | copy-start | bytes 100
  23.1 12.5 %collective-permute-start.3 = (bf16[128,128]{1,0:T(8,128)(2,1)S(1)}, bf16[128,128]{1,0:T(8,128)(2,1)S(1)}, u32[]{:S(2)}, u32[]{:S(2)}) collective-permute-start(bf16[128,128]{1,0:T(8,128)(2,1)S(1)} %bitcast.16), channel_id=1, source_target_pairs={{17,32},{46,16},{31,40},{42,24},{49,64},{78,48},{63,72},{74,56},{8... | collective-permute-start | bytes 98312 | tf_op jit(solution)/shard_map/ppermute | solution.py:227
  24.4 11.2 %collective-permute-start.2 = (bf16[128,128]{1,0:T(8,128)(2,1)S(1)}, bf16[128,128]{1,0:T(8,128)(2,1)S(1)}, u32[]{:S(2)}, u32[]{:S(2)}) collective-permute-start(bf16[128,128]{1,0:T(8,128)(2,1)S(1)} %bitcast.17), channel_id=1, source_target_pairs={{1,16},{30,0},{15,24},{26,8},{33,48},{62,32},{47,56},{58,40},{65,8... | collective-permute-start | bytes 98312 | tf_op jit(solution)/shard_map/ppermute | solution.py:227

commit v6 on v5

--- a/solution.py
+++ b/solution.py
@@ -9,7 +9,7 @@
 NEAR = 2
 CAP = 2
 REACH = 2 * NEAR + 1
-NEXT = ((0, 1), (1, 7))
+NEXT = ((0, 6), (1, 7))
 PREVIOUS = ((1, 6), (1, 2))
 EMPTY = 64
 

time: 36.8 us -> 36.8 us (level)
  no operation moved by 1% of the time
where the time goes in v6:
time: 36.8 us; the launch traced here: 36.4 us
  starting transfers between devices  22.5 us (61%)
  waiting for transfers between devices  8.79 us (24%)
  Pallas kernels  4.36 us (12%)
  between operations  0.78 us (2%)
    all_to_all x1, starting transfers between devices, shards(): lax.all_to_all(send, ('horiz', 'lev'), 0, 0, axis_index_groups=pairs, til...  16.6 us
    ppermute x2, waiting for transfers between devices, swap(): return lax.ppermute(own, ('horiz', 'lev'), pairs)  8.79 us
    ppermute x2, starting transfers between devices, swap(): return lax.ppermute(own, ('horiz', 'lev'), pairs)  2.58 us
    pallas_call x1, Pallas kernels, shards(): pl.pallas_call(prep_kernel, out_shape=(shape((128, 128), bf16), shape((12...  2.48 us
    ppermute x1, starting transfers between devices, shards(): below = lax.ppermute(up, 'lev', [(i, i + 1) for i in range(levels - 1)])  1.98 us
    ppermute x1, starting transfers between devices, shards(): above = lax.ppermute(down, 'lev', [(i + 1, i) for i in range(levels - 1)])  1.29 us
    pallas_call x1, Pallas kernels, shards(): pl.pallas_call(column_kernel, out_shape=(shape(atm_state.shape, f32), sha...  1.08 us
    pallas_call x1, Pallas kernels, shards(): pl.pallas_call(surface_kernel, out_shape=(shape(atm_state.shape, f32), sh...  0.8 us
  transfers between devices with their start and end apart: 5, of which 1 were waited for; matrix products, arithmetic and copies ran while one was open for 0% of the time, Pallas kernels for 3%

profile of v6, /device:TPU:32, one launch (start us, length us, event | category | flops | bytes accessed | tf_op | source)
XLA Modules:
  0.0 36.4 jit_solution(12864645229669890548)
XLA Ops:
  0.6 0.0 copy-start
  0.6 2.5 %shard_map.140 = (bf16[128,128]{1,0:T(8,128)(2,1)}, f32[12,16,128]{2,1,0:T(8,128)}, f32[12,16,128]{2,1,0:T(8,128)}) custom-call(s32[10]{0:T(128)} %ocean_src_hbm.1, s32[10]{0:T(128)} %ocean_dst_hbm.1, s32[10]{0:T(128)} %atmos_src_hbm.1, s32[10]{0:T(128)} %atmos_dst_hbm.1, f32[4,2,16,256]{3,2,1,0:T(8,128)} %atm.1, f32[128,128]{1,0:T(8,128)} %bitcast.14, ...), custom_call_target="tpu_custom_call" | custom-call | tf_op jit(solution)/shard_map/pallas_call | solution.py:191
  3.1 0.0 copy-start.1
  3.1 0.0 copy-start.2
  3.2 16.6 %all-to-all-start = ((bf16[16,8,128]{2,1,0:T(8,128)(2,1)}), bf16[16,8,128]{2,1,0:T(8,128)(2,1)S(1)}, u32[]{:S(2)}, u32[]{:S(2)}) async-start(bf16[16,8,128]{2,1,0:T(8,128)(2,1)} %bitcast.21), calls=%async_computation | async-start | bytes 65536 | tf_op jit(solution)/shard_map/all_to_all | solution.py:217
  19.8 2.0 %collective-permute-start = (f32[12,16,128]{2,1,0:T(8,128)}, f32[12,16,128]{2,1,0:T(8,128)S(1)}, u32[]{:S(2)}, u32[]{:S(2)}) collective-permute-start(f32[12,16,128]{2,1,0:T(8,128)} %get-tuple-element.11), channel_id=1, source_target_pairs={{0,1},{1,2},{2,3},{3,4},{4,5},{5,6},{6,7},{8,9},{9,10},{10,11},{11... | collective-permute-start | bytes 294920 | tf_op jit(solution)/shard_map/ppermute | solution.py:231
  21.8 1.3 %collective-permute-start.1 = (f32[12,16,128]{2,1,0:T(8,128)}, f32[12,16,128]{2,1,0:T(8,128)S(1)}, u32[]{:S(2)}, u32[]{:S(2)}) collective-permute-start(f32[12,16,128]{2,1,0:T(8,128)} %get-tuple-element.12), channel_id=1, source_target_pairs={{1,0},{2,1},{3,2},{4,3},{5,4},{6,5},{7,6},{9,8},{10,9},{11,10},{12... | collective-permute-start | bytes 294920 | tf_op jit(solution)/shard_map/ppermute | solution.py:232
  23.1 0.0 all-to-all-done
  23.1 0.0 copy-start.4
  23.1 0.0 copy-start.3
  23.1 1.3 %collective-permute-start.3 = (bf16[128,128]{1,0:T(8,128)(2,1)S(1)}, bf16[128,128]{1,0:T(8,128)(2,1)S(1)}, u32[]{:S(2)}, u32[]{:S(2)}) collective-permute-start(bf16[128,128]{1,0:T(8,128)(2,1)S(1)} %bitcast.16), channel_id=1, source_target_pairs={{22,32},{46,16},{31,40},{42,24},{54,64},{78,48},{63,72},{74,56},{8... | collective-permute-start | bytes 98312 | tf_op jit(solution)/shard_map/ppermute | solution.py:227
  24.4 1.3 %collective-permute-start.2 = (bf16[128,128]{1,0:T(8,128)(2,1)S(1)}, bf16[128,128]{1,0:T(8,128)(2,1)S(1)}, u32[]{:S(2)}, u32[]{:S(2)}) collective-permute-start(bf16[128,128]{1,0:T(8,128)(2,1)S(1)} %bitcast.17), channel_id=1, source_target_pairs={{6,16},{30,0},{15,24},{26,8},{38,48},{62,32},{47,56},{58,40},{70,8... | collective-permute-start | bytes 98312 | tf_op jit(solution)/shard_map/ppermute | solution.py:227
  25.7 0.0 collective-permute-done.below
  25.7 0.0 collective-permute-done.1.above
  25.7 0.0 copy-done
  25.7 0.0 copy-done.1
  25.7 0.0 copy-done.2
  25.8 0.0 copy-done.4
  25.8 0.0 copy-done.3
  25.8 1.1 %shard_map.141 = (f32[4,2,16,256]{3,2,1,0:T(8,128)}, f32[128,128]{1,0:T(8,128)}, f32[16,256]{1,0:T(8,128)S(1)}, f32[64,128]{1,0:T(8,128)S(1)}) custom-call(f32[2,4]{1,0:T(2,128)S(1)} %bitcast.19, f32[2,2]{1,0:T(2,128)S(1)} %copy-done.4, f32[4,2,16,256]{3,2,1,0:T(8,128)S(1)} %copy-done, f32[128,128]{1,0:T(8,128)S(1)} %bitcast.15, f32[16,16]{1,0:T(8,128)S(1)} %copy-done.2, ...), custom_call_target="tpu_custom_call" | custom-call | tf_op jit(solution)/shard_map/pallas_call | solution.py:233
  26.9 8.8 %collective-permute-done.3.first = bf16[128,128]{1,0:T(8,128)(2,1)S(1)} collective-permute-done((bf16[128,128]{1,0:T(8,128)(2,1)S(1)}, bf16[128,128]{1,0:T(8,128)(2,1)S(1)}, u32[]{:S(2)}, u32[]{:S(2)}) %collective-permute-start.3) | collective-permute-done | bytes 32800 | tf_op jit(solution)/shard_map/ppermute | solution.py:227
  35.6 0.0 collective-permute-done.2.second
  35.6 0.8 %shard_map.142 = (f32[4,2,16,256]{3,2,1,0:T(8,128)}, f32[128,128]{1,0:T(8,128)}) custom-call(f32[4,2,16,256]{3,2,1,0:T(8,128)} %get-tuple-element.13.atm_in, f32[128,128]{1,0:T(8,128)} %get-tuple-element.14.ocean_in, f32[16,256]{1,0:T(8,128)S(1)} %get-tuple-element.15.atm_base, ...), custom_call_target="tpu_custom_call", output_to_operand_aliasing={{0}: (0, {}), {1}: (1, {})} | custom-call | tf_op jit(solution)/shard_map/pallas_call | solution.py:250
Async XLA Ops:
  0.6 25.1 %copy-start = (f32[4,2,16,256]{3,2,1,0:T(8,128)S(1)}, f32[4,2,16,256]{3,2,1,0:T(8,128)}, u32[]{:S(2)}) copy-start(f32[4,2,16,256]{3,2,1,0:T(8,128)} %atm.1) | copy-start | bytes 393220
  3.1 22.6 %copy-start.1 = (f32[2,2,4096]{2,1,0:T(2,128)S(1)}, f32[2,2,4096]{2,1,0:T(2,128)}, u32[]{:S(2)}) copy-start(f32[2,2,4096]{2,1,0:T(2,128)} %param.16) | copy-start | bytes 196612
  3.1 22.6 %copy-start.2 = (f32[16,16]{1,0:T(8,128)S(1)}, f32[16,16]{1,0:T(8,128)}, u32[]{:S(2)}) copy-start(f32[16,16]{1,0:T(8,128)} %operator.1) | copy-start | bytes 3076
  3.2 19.9 %all-to-all-start = ((bf16[16,8,128]{2,1,0:T(8,128)(2,1)}), bf16[16,8,128]{2,1,0:T(8,128)(2,1)S(1)}, u32[]{:S(2)}, u32[]{:S(2)}) async-start(bf16[16,8,128]{2,1,0:T(8,128)(2,1)} %bitcast.21), calls=%async_computation | async-start | bytes 65536 | tf_op jit(solution)/shard_map/all_to_all | solution.py:217
  19.8 5.9 %collective-permute-start = (f32[12,16,128]{2,1,0:T(8,128)}, f32[12,16,128]{2,1,0:T(8,128)S(1)}, u32[]{:S(2)}, u32[]{:S(2)}) collective-permute-start(f32[12,16,128]{2,1,0:T(8,128)} %get-tuple-element.11), channel_id=1, source_target_pairs={{0,1},{1,2},{2,3},{3,4},{4,5},{5,6},{6,7},{8,9},{9,10},{10,11},{11... | collective-permute-start | bytes 294920 | tf_op jit(solution)/shard_map/ppermute | solution.py:231
  21.8 3.9 %collective-permute-start.1 = (f32[12,16,128]{2,1,0:T(8,128)}, f32[12,16,128]{2,1,0:T(8,128)S(1)}, u32[]{:S(2)}, u32[]{:S(2)}) collective-permute-start(f32[12,16,128]{2,1,0:T(8,128)} %get-tuple-element.12), channel_id=1, source_target_pairs={{1,0},{2,1},{3,2},{4,3},{5,4},{6,5},{7,6},{9,8},{10,9},{11,10},{12... | collective-permute-start | bytes 294920 | tf_op jit(solution)/shard_map/ppermute | solution.py:232
  23.1 2.7 %copy-start.4 = (f32[2,2]{1,0:T(2,128)S(1)}, f32[2,2]{1,0:T(2,128)}, u32[]{:S(2)}) copy-start(f32[2,2]{1,0:T(2,128)} %ocean_mixing.1) | copy-start | bytes 52
  23.1 2.7 %copy-start.3 = (f32[4,2]{0,1:T(2,128)S(1)}, f32[4,2]{0,1:T(2,128)}, u32[]{:S(2)}) copy-start(f32[4,2]{0,1:T(2,128)} %param.14) | copy-start | bytes 100
  23.1 12.5 %collective-permute-start.3 = (bf16[128,128]{1,0:T(8,128)(2,1)S(1)}, bf16[128,128]{1,0:T(8,128)(2,1)S(1)}, u32[]{:S(2)}, u32[]{:S(2)}) collective-permute-start(bf16[128,128]{1,0:T(8,128)(2,1)S(1)} %bitcast.16), channel_id=1, source_target_pairs={{22,32},{46,16},{31,40},{42,24},{54,64},{78,48},{63,72},{74,56},{8... | collective-permute-start | bytes 98312 | tf_op jit(solution)/shard_map/ppermute | solution.py:227
  24.4 11.2 %collective-permute-start.2 = (bf16[128,128]{1,0:T(8,128)(2,1)S(1)}, bf16[128,128]{1,0:T(8,128)(2,1)S(1)}, u32[]{:S(2)}, u32[]{:S(2)}) collective-permute-start(bf16[128,128]{1,0:T(8,128)(2,1)S(1)} %bitcast.17), channel_id=1, source_target_pairs={{6,16},{30,0},{15,24},{26,8},{38,48},{62,32},{47,56},{58,40},{70,8... | collective-permute-start | bytes 98312 | tf_op jit(solution)/shard_map/ppermute | solution.py:227
